TPU v7x, 512 devices: a whole 4x4x16 slice. The times are simulated.
512 devices in a mesh: lon: 64 (over y, z_lo, core), rad: 8 (over z_hi, x).
Axes of the slice: x: 4, y: 4, z: 16 (z_hi: 2, z_lo: 8; z = z_hi * 8 + z_lo), core: 2. Of those that a mesh axis runs over, the one named last changes fastest.
Arguments:
- logvisc: float32 [96, 256, 512], P('rad', 'lon'), may hold values from -1 to 1
- momentum: float32 [96, 256, 512], P('rad', 'lon'), may hold values from -6 to 6
- displacement: float32 [3, 96, 256, 512], P(None, 'rad', 'lon'), may hold values from -6 to 6
- ice_history: float32 [8, 256, 512], P(None, 'lon'), may hold values from -6 to 6
- load_steps: int32 [2], replicated, may hold values from 0 to 7
- site_cells: int32 [768], P('lon'), may hold values from 0 to 131071
- observed: float32 [3, 768], P(None, 'lon'), may hold values from -6 to 6
- site_weight: float32 [3, 768], P(None, 'lon'), may hold values from 2 to 6
Outputs:
- new_logvisc: float32 [96, 256, 512], P('rad', 'lon')
- half_momentum: float32 [96, 256, 512], P('rad', 'lon')
- misfit: float32 [1], replicated
Inputs may be any that keep to these rules, and one draw needn't show every extreme that they name: site_cells holds lon * 512 + lat of the surface cell where the site stands. load_steps indexes the first dimension of ice_history.
All inputs are finite; a program needn't handle non-finite values.
Results may differ from a plain program's by a relative error of at most 0.0003.
Values sent between devices are 32-bit elements; how exact they have to be, the bound alone decides.
A program may use at most 64 MiB of HBM per device.

v0:
```python
import math

import jax
import jax.numpy as jnp
from jax import lax
from jax.sharding import PartitionSpec as P

RELAX = 2


RELAX_RATE = 0.05
KERNEL_WIDTH = 0.1
KERNEL_WAVE = 40.0
PRIOR_WEIGHT = 0.1
LOAD_FACTOR = 1.0


def extended(block, sides, width, periodic):
    for axis, dim in sides:
        count = lax.axis_size(axis)
        forward = [(i, i + 1) for i in range(count - 1)]
        if periodic:
            forward.append((count - 1, 0))
        backward = [(target, source) for source, target in forward]
        low = lax.ppermute(
            lax.slice_in_dim(block, block.shape[dim] - width, None, axis=dim), axis, forward
        )
        high = lax.ppermute(lax.slice_in_dim(block, 0, width, axis=dim), axis, backward)
        block = jnp.concatenate([low, block, high], axis=dim)
    return block


def harmonic(center_fluid, other_fluid):
    summed = center_fluid + other_fluid
    coeff = 2.0 * center_fluid * other_fluid / summed
    slope = 2.0 * other_fluid * other_fluid / (summed * summed)
    return (coeff, slope)


def neighbours(padded):
    return [
        padded[:, 2:, 1:-1, 1:-1],
        padded[:, :-2, 1:-1, 1:-1],
        padded[:, 1:-1, 2:, 1:-1],
        padded[:, 1:-1, :-2, 1:-1],
        padded[:, 1:-1, 1:-1, 2:],
        padded[:, 1:-1, 1:-1, :-2],
    ]


def middle(padded):
    return padded[:, 1:-1, 1:-1, 1:-1]


def apply_operator(field_pad, fluid_pad):
    fluid_mid = middle(fluid_pad)
    field_mid = middle(field_pad)
    total = jnp.zeros(field_mid.shape, jnp.float32)
    for fluid_side, field_side in zip(neighbours(fluid_pad), neighbours(field_pad)):
        coeff, slope = harmonic(fluid_mid, fluid_side)
        total = total + coeff * (field_side - field_mid)
    return total


def fluid_gradient(state_pad, adjoint_pad, fluid_pad):
    fluid_mid = middle(fluid_pad)
    state_mid = middle(state_pad)
    adjoint_mid = middle(adjoint_pad)
    total = jnp.zeros(fluid_mid.shape, jnp.float32)
    for fluid_side, state_side, adjoint_side in zip(
        neighbours(fluid_pad), neighbours(state_pad), neighbours(adjoint_pad)
    ):
        coeff, slope = harmonic(fluid_mid, fluid_side)
        product = jnp.sum(
            (state_side - state_mid) * (adjoint_side - adjoint_mid), axis=0, keepdims=True
        )
        total = total + slope * product
    return -RELAX_RATE * total


def extend(field):
    layered = extended(field, (("rad", 1),), 1, False)
    beside_all = extended(layered, (("lon", 2),), 1, True)
    return jnp.pad(beside_all, ((0, 0), (0, 0), (0, 0), (1, 1)))


def cell_features(lon_index, lat_index, total_lon, total_lat):
    theta = math.pi * (lat_index.astype(jnp.float32) + 0.5) / total_lat
    phi = 2.0 * math.pi * lon_index.astype(jnp.float32) / total_lon
    upward = jnp.broadcast_to(jnp.cos(theta)[None, :], (phi.shape[0], theta.shape[0]))
    eastern = jnp.sin(theta)[None, :] * jnp.cos(phi)[:, None]
    northern = jnp.sin(theta)[None, :] * jnp.sin(phi)[:, None]
    return jnp.stack([upward, eastern, northern]).reshape(3, -1)


def site_features(cells, total_lon, total_lat):
    lon_index = cells // total_lat
    lat_index = cells % total_lat
    theta = math.pi * (lat_index.astype(jnp.float32) + 0.5) / total_lat
    phi = 2.0 * math.pi * lon_index.astype(jnp.float32) / total_lon
    return jnp.stack(
        [jnp.cos(theta), jnp.sin(theta) * jnp.cos(phi), jnp.sin(theta) * jnp.sin(phi)], axis=1
    )


def kernel(site_feats, cell_feats):
    cosine = (
        site_feats[:, 0:1] * cell_feats[0:1]
        + site_feats[:, 1:2] * cell_feats[1:2]
        + site_feats[:, 2:3] * cell_feats[2:3]
    )
    chord = 2.0 - 2.0 * cosine
    return 1.0 / (1.0 + chord / KERNEL_WIDTH) + 0.5 * jnp.cos(KERNEL_WAVE * chord)


def group_size(total_rows, unit, cells):
    blocks = total_rows // unit
    chosen = 1
    for candidate in range(1, 9):
        if blocks % candidate == 0 and candidate * unit * cells <= 1048576:
            chosen = candidate
    return chosen * unit


def predict_rows(feats, cell_feats, surface_flat, unit):
    size = group_size(feats.shape[0], unit, cell_feats.shape[1])
    blocks = feats.reshape(-1, size, 3)

    def one_block(block):
        weights = kernel(block, cell_feats)
        return jnp.einsum(
            "sm,cm->sc",
            weights,
            surface_flat,
            precision=lax.Precision.HIGHEST,
            preferred_element_type=jnp.float32,
        )

    return lax.map(one_block, blocks).reshape(-1, 3)


def body(
    logvisc, momentum, displacement, ice_history, load_steps, site_cells, observed, site_weight
):
    rad_rows = logvisc.shape[0]
    lon_cols = logvisc.shape[1]
    lat_cells = logvisc.shape[2]
    site_rows = site_cells.shape[0]
    total_rad = rad_rows * lax.axis_size("rad")
    total_lon = lon_cols * lax.axis_size("lon")
    lat_width = lat_cells // lax.axis_size("rad")
    scale = 1.0 / math.sqrt(total_lon * lat_cells)
    rad_global = lax.axis_index("rad") * rad_rows + jnp.arange(rad_rows)
    lon_global = lax.axis_index("lon") * lon_cols + jnp.arange(lon_cols)
    depth_weight = jnp.exp(4.0 * (rad_global.astype(jnp.float32) - (total_rad - 1)) / total_rad)
    top_row = (rad_global == total_rad - 1).astype(jnp.float32)[None, :, None, None]
    upward = (jnp.arange(3) == 0).astype(jnp.float32)[:, None, None, None]
    fluidity = jnp.exp(-logvisc)
    fluid_pad = extend(fluidity[None])
    state = displacement
    saved = []
    for level in range(RELAX):
        padded = extend(state)
        saved.append(padded)
        load = lax.dynamic_index_in_dim(ice_history, load_steps[level], 0, keepdims=False)
        state = (
            state
            + RELAX_RATE * apply_operator(padded, fluid_pad)
            - LOAD_FACTOR * upward * top_row * load[None, None]
        )
    column = jnp.sum(depth_weight[None, :, None, None] * state, axis=1)
    lat_start = lax.axis_index("rad") * lat_width
    lat_band = lat_start + jnp.arange(lat_width)
    whole_column = lax.psum(column, "rad")
    band = lax.dynamic_slice_in_dim(whole_column, lat_start, lat_width, 2)
    band_feats = cell_features(lon_global, lat_band, total_lon, lat_cells)
    own_feats = site_features(site_cells, total_lon, lat_cells)
    all_feats = lax.all_gather(own_feats, "lon", axis=0, tiled=True)
    band_flat = band.reshape(3, -1)
    partial_pred = lax.psum_scatter(
        predict_rows(all_feats, band_feats, band_flat, site_rows) * scale,
        "lon",
        scatter_dimension=0,
        tiled=True,
    )
    predicted = lax.psum(partial_pred, "rad").T
    weighted = site_weight * (predicted - observed)
    misfit = lax.psum(jnp.sum(weighted * weighted), "lon") / (3 * total_lon // lon_cols * site_rows)
    adjoint_cells = cell_features(lon_global, jnp.arange(lat_cells), total_lon, lat_cells)
    packet = jnp.concatenate([own_feats, (site_weight * weighted).T], axis=1)
    piece = lax.all_gather(packet, "lon", axis=0, tiled=True)
    size = group_size(piece.shape[0], site_rows, adjoint_cells.shape[1])
    blocks = piece.reshape(-1, size, 6)

    def add_block(running, block):
        weights = kernel(block[:, :3], adjoint_cells)
        return (
            running
            + jnp.einsum(
                "sc,sm->cm",
                block[:, 3:],
                weights,
                precision=lax.Precision.HIGHEST,
                preferred_element_type=jnp.float32,
            ),
            None,
        )

    running, unused = lax.scan(
        add_block, jnp.zeros((3, adjoint_cells.shape[1]), jnp.float32), blocks
    )
    surface_adjoint = (running * scale).reshape(3, lon_cols, lat_cells)
    adjoint = depth_weight[None, :, None, None] * surface_adjoint[:, None]
    gradient_fluid = jnp.zeros((1, rad_rows, lon_cols, lat_cells), jnp.float32)
    for level in range(RELAX - 1, -1, -1):
        adjoint_pad = extend(adjoint)
        gradient_fluid = gradient_fluid + fluid_gradient(saved[level], adjoint_pad, fluid_pad)
        if level > 0:
            adjoint = adjoint + RELAX_RATE * apply_operator(adjoint_pad, fluid_pad)
    gradient = -fluidity * gradient_fluid[0] + PRIOR_WEIGHT * logvisc
    half_momentum = momentum - 0.5 * gradient
    new_logvisc = logvisc + half_momentum
    return (new_logvisc, half_momentum, misfit.reshape(1))


def solution(mesh):
    return jax.shard_map(
        body,
        mesh=mesh,
        in_specs=(
            P("rad", "lon", None),
            P("rad", "lon", None),
            P(None, "rad", "lon", None),
            P(None, "lon", None),
            P(),
            P("lon"),
            P(None, "lon"),
            P(None, "lon"),
        ),
        out_specs=(P("rad", "lon", None), P("rad", "lon", None), P()),
        check_vma=False,
    )
```

profile of v0, /device:TPU:6, one launch (start us, length us, event | category | flops | bytes accessed | tf_op | source)
XLA Modules:
  0.0 1209.8 jit_solution(8901349295984895374)
XLA Ops:
  0.6 0.8 fusion.143
  1.4 15.6 %collective-permute-start.3 = (f32[3,1,4,512]{3,2,1,0:T(4,128)S(1)}, f32[3,1,4,512]{3,2,1,0:T(4,128)S(1)}, u32[]{:S(2)}, u32[]{:S(2)}) collective-permute-start(f32[3,1,4,512]{3,2,1,0:T(4,128)S(1)} %get-tuple-element.153), channel_id=1, source_target_pairs={{0,1},{1,2},{2,3},{3,4},{4,5},{5,6},{6,7},{8,9},{9,10},{10,11},{11... | collective-permute-start | bytes 73736 | tf_op jit(solution)/shard_map/ppermute | solution.py:25
  17.1 1.9 collective-permute-start.1
  19.1 14.9 %collective-permute-start.2 = (f32[1,1,4,512]{3,2,1,0:T(4,128)S(1)}, f32[1,1,4,512]{3,2,1,0:T(4,128)S(1)}, u32[]{:S(2)}, u32[]{:S(2)}) collective-permute-start(f32[1,1,4,512]{3,2,1,0:T(4,128)S(1)} %get-tuple-element.163), channel_id=1, source_target_pairs={{0,1},{1,2},{2,3},{3,4},{4,5},{5,6},{6,7},{8,9},{9,10},{10,11},{11... | collective-permute-start | bytes 24584 | tf_op jit(solution)/shard_map/ppermute | solution.py:25
  34.0 1.9 collective-permute-start
  42.3 1.3 dynamic-slice_bitcast_fusion
  44.2 6.1 collective-permute-done
  50.4 1.9 collective-permute-start.6
  52.3 12.4 %collective-permute-start.4 = (f32[1,14,1,512]{3,2,1,0:T(1,128)S(1)}, f32[1,14,1,512]{3,2,1,0:T(1,128)S(1)}, u32[]{:S(2)}, u32[]{:S(2)}) collective-permute-start(f32[1,14,1,512]{3,2,1,0:T(1,128)S(1)} %get-tuple-element.160), channel_id=1, source_target_pairs={{8,0},{16,8},{24,16},{32,24},{40,32},{48,40},{56,48},{64,56},{72,6... | collective-permute-start | bytes 86024 | tf_op jit(solution)/shard_map/ppermute | solution.py:28
  65.0 1.9 collective-permute-start.7
  66.9 12.4 %collective-permute-start.5 = (f32[3,14,1,512]{3,2,1,0:T(1,128)S(1)}, f32[3,14,1,512]{3,2,1,0:T(1,128)S(1)}, u32[]{:S(2)}, u32[]{:S(2)}) collective-permute-start(f32[3,14,1,512]{3,2,1,0:T(1,128)S(1)} %get-tuple-element.146), channel_id=1, source_target_pairs={{8,0},{16,8},{24,16},{32,24},{40,32},{48,40},{56,48},{64,56},{72,6... | collective-permute-start | bytes 258056 | tf_op jit(solution)/shard_map/ppermute | solution.py:28
  80.3 1.2 collective-permute-done.5
  81.5 0.8 select_maximum_fusion.12
  82.4 0.9 multiply_subtract_fusion.6
  83.3 8.5 collective-permute-start.9
  91.8 1.9 collective-permute-start.8
  93.8 112.6 %all-gather = f32[64,12,3]{1,2,0:T(4,128)S(1)} all-gather(f32[1,12,3]{1,2,0:T(4,128)S(1)} %maximum_bitcast_fusion.1), channel_id=1, replica_groups=mesh['lon'=64,'rad'=8] {'lon'}, dimensions={0}, use_global_device_ids=true | all-gather | bytes 9360 | tf_op jit(solution)/shard_map/all_gather | solution.py:178
  207.1 1.3 dynamic-slice
  209.6 2.2 collective-permute-start.11
  211.8 12.0 collective-permute-start.10
  224.1 1.8 collective-permute-done.10
  225.9 1.6 select_maximum_fusion.8
  227.6 1.5 multiply_reduce_fusion.6
  229.1 65.8 %psum.21 = f32[3,4,512]{2,1,0:T(4,128)S(1)} all-reduce(f32[3,4,512]{2,1,0:T(4,128)} %multiply_reduce_fusion.6), channel_id=1, replica_groups=mesh['lon'=64,'rad'=8] {'rad'}, use_global_device_ids=true, to_apply=%region_1.2 | all-reduce | flops 6144 | bytes 49152 | tf_op jit(solution)/shard_map/psum | solution.py:174
  295.6 11.0 while.21
  297.0 0.8 constant_dynamic-slice_fusion.5
  298.4 0.8 constant_dynamic-slice_fusion.5
  299.7 0.8 constant_dynamic-slice_fusion.5
  301.1 0.8 constant_dynamic-slice_fusion.5
  302.5 0.8 constant_dynamic-slice_fusion.5
  303.9 0.8 constant_dynamic-slice_fusion.5
  305.2 0.8 constant_dynamic-slice_fusion.5
  306.8 422.6 %all-reduce.5 = f32[768,3]{0,1:T(4,128)S(1)} all-reduce(f32[768,3]{0,1:T(4,128)S(1)} %mul.762), channel_id=2, replica_groups=mesh['lon'=64,'rad'=8] {'lon'}, use_global_device_ids=true, to_apply=%region_4.5.clone | all-reduce | flops 2304 | bytes 18432
  729.5 35.5 %psum.22 = f32[3,12]{1,0:T(4,128)S(1)} all-reduce(f32[3,12]{1,0:T(4,128)S(1)} %dynamic-slice_bitcast_fusion.2), channel_id=1, replica_groups=mesh['lon'=64,'rad'=8] {'rad'}, use_global_device_ids=true, to_apply=%region_5.6 | all-reduce | flops 36 | bytes 288 | tf_op jit(solution)/shard_map/psum | solution.py:186
  766.3 113.3 %all-gather.1 = f32[64,12,6]{1,2,0:T(8,128)S(1)} all-gather(f32[1,12,6]{1,2,0:T(8,128)S(1)} %maximum_bitcast_fusion), channel_id=1, replica_groups=mesh['lon'=64,'rad'=8] {'lon'}, dimensions={0}, use_global_device_ids=true | all-gather | bytes 18720 | tf_op jit(solution)/shard_map/all_gather | solution.py:191
  880.4 28.1 %while.22 = (s32[]{:T(128)}, f32[3,2048]{1,0:T(4,128)S(1)}, f32[8,96,6]{1,0,2:T(8,128)S(1)}, f32[3,2048]{1,0:T(4,128)S(1)}, s32[]{:T(128)}, /*index=5*/s32[]{:T(128)}) while((s32[]{:T(128)}, f32[3,2048]{1,0:T(4,128)S(1)}, f32[8,96,6]{1,0,2:T(8,128)S(1)}, f32[3,2048]{1,0:T(4,128)S(1)}, s32[]{:T(128)}, /*index=5*/s32[]{:T(128)}) %tuple.102), condition=%wide.region_7.8_spmd.clone, body=%wide.region_6.7_spmd.clone.sunk | while | flops 9646083 | bytes 146267 | solution.py:209
  880.5 3.4 convolution_add_fusion.2
  884.0 3.4 convolution_add_fusion.2
  887.5 3.4 convolution_add_fusion.2
  891.0 3.4 convolution_add_fusion.2
  894.5 3.4 convolution_add_fusion.2
  898.0 3.4 convolution_add_fusion.2
  901.6 3.4 convolution_add_fusion.2
  905.1 3.4 convolution_add_fusion.2
  908.6 0.8 broadcast_multiply_fusion
  909.4 12.8 %collective-permute-start.13 = (f32[3,1,4,512]{3,2,1,0:T(4,128)S(1)}, f32[3,1,4,512]{3,2,1,0:T(4,128)S(1)}, u32[]{:S(2)}, u32[]{:S(2)}) collective-permute-start(f32[3,1,4,512]{3,2,1,0:T(4,128)S(1)} %get-tuple-element.149), channel_id=1, source_target_pairs={{0,1},{1,2},{2,3},{3,4},{4,5},{5,6},{6,7},{8,9},{9,10},{10,11},{11... | collective-permute-start | bytes 73736 | tf_op jit(solution)/shard_map/ppermute | solution.py:25
  922.2 1.9 collective-permute-start.12
  924.1 14.6 %collective-permute-done.12 = f32[3,1,4,512]{3,2,1,0:T(4,128)S(1)} collective-permute-done((f32[3,1,4,512]{3,2,1,0:T(4,128)S(1)}, f32[3,1,4,512]{3,2,1,0:T(4,128)S(1)}, u32[]{:S(2)}, u32[]{:S(2)}) %collective-permute-start.12) | collective-permute-done | bytes 24608 | tf_op jit(solution)/shard_map/ppermute | solution.py:28
  938.7 0.8 pad_maximum_fusion.39
  939.5 1.9 collective-permute-start.15
  941.5 12.4 %collective-permute-start.14 = (f32[3,14,1,512]{3,2,1,0:T(1,128)}, f32[3,14,1,512]{3,2,1,0:T(1,128)}, u32[]{:S(2)}, u32[]{:S(2)}) collective-permute-start(f32[3,14,1,512]{3,2,1,0:T(1,128)} %get-tuple-element.142), channel_id=1, source_target_pairs={{8,0},{16,8},{24,16},{32,24},{40,32},{48,40},{56,48},{64,56},{72,6... | collective-permute-start | bytes 258056 | tf_op jit(solution)/shard_map/ppermute | solution.py:28
  953.8 210.9 %psum.23 = f32[]{:T(128)} all-reduce(f32[]{:T(128)} %get-tuple-element.169), channel_id=1, replica_groups=mesh['lon'=64,'rad'=8] {'lon'}, use_global_device_ids=true, to_apply=%region_21.22 | all-reduce | flops 1 | bytes 8 | tf_op jit(solution)/shard_map/psum | solution.py:188
  1165.4 1.9 select_maximum_fusion.4
  1167.4 1.7 multiply_add_fusion
  1169.1 1.9 collective-permute-start.17
  1171.1 3.9 collective-permute-start.16
  1175.0 0.9 multiply_reduce_fusion.5
  1175.9 11.7 collective-permute-done.16
  1187.7 1.9 collective-permute-start.19
  1189.7 12.5 %collective-permute-start.18 = (f32[3,14,1,512]{3,2,1,0:T(1,128)S(1)}, f32[3,14,1,512]{3,2,1,0:T(1,128)S(1)}, u32[]{:S(2)}, u32[]{:S(2)}) collective-permute-start(f32[3,14,1,512]{3,2,1,0:T(1,128)S(1)} %get-tuple-element.140), channel_id=1, source_target_pairs={{8,0},{16,8},{24,16},{32,24},{40,32},{48,40},{56,48},{64,56},{72,6... | collective-permute-start | bytes 258056 | tf_op jit(solution)/shard_map/ppermute | solution.py:28
  1202.2 1.7 multiply_reduce_fusion.3
  1204.3 0.8 fusion.72
  1205.1 0.8 select_maximum_fusion
  1207.4 1.2 fusion.134
  (267 shorter events, 16.8 us)
Async XLA Ops:
  0.6 18.4 %copy-start.10 = (f32[12,4,512]{2,1,0:T(4,128)S(1)}, f32[12,4,512]{2,1,0:T(4,128)}, u32[]{:S(2)}) copy-start(f32[12,4,512]{2,1,0:T(4,128)} %param.12) | copy-start | bytes 294916
  1.4 63.3 %collective-permute-start.3 = (f32[3,1,4,512]{3,2,1,0:T(4,128)S(1)}, f32[3,1,4,512]{3,2,1,0:T(4,128)S(1)}, u32[]{:S(2)}, u32[]{:S(2)}) collective-permute-start(f32[3,1,4,512]{3,2,1,0:T(4,128)S(1)} %get-tuple-element.153), channel_id=1, source_target_pairs={{0,1},{1,2},{2,3},{3,4},{4,5},{5,6},{6,7},{8,9},{9,10},{10,11},{11... | collective-permute-start | bytes 73736 | tf_op jit(solution)/shard_map/ppermute | solution.py:25
  17.1 47.7 %collective-permute-start.1 = (f32[3,1,4,512]{3,2,1,0:T(4,128)S(1)}, f32[3,1,4,512]{3,2,1,0:T(4,128)S(1)}, u32[]{:S(2)}, u32[]{:S(2)}) collective-permute-start(f32[3,1,4,512]{3,2,1,0:T(4,128)S(1)} %get-tuple-element.154), channel_id=1, source_target_pairs={{1,0},{2,1},{3,2},{4,3},{5,4},{6,5},{7,6},{9,8},{10,9},{11,10},{12... | collective-permute-start | bytes 73736 | tf_op jit(solution)/shard_map/ppermute | solution.py:28
  19.1 16.9 %copy-start.55 = (s32[2]{0:T(128)S(1)}, s32[2]{0:T(128)}, u32[]{:S(2)}) copy-start(s32[2]{0:T(128)} %param.16) | copy-start | bytes 28
  19.1 20.3 %copy-start.60 = (s32[12]{0:T(128)S(1)}, s32[12]{0:T(128)}, u32[]{:S(2)}) copy-start(s32[12]{0:T(128)} %param.17) | copy-start | bytes 148
  19.1 45.6 %copy-start = (f32[3,12,4,512]{3,2,1,0:T(4,128)S(1)}, f32[3,12,4,512]{3,2,1,0:T(4,128)}, u32[]{:S(2)}) copy-start(f32[3,12,4,512]{3,2,1,0:T(4,128)} %param.14) | copy-start | bytes 884740
  19.1 25.1 %collective-permute-start.2 = (f32[1,1,4,512]{3,2,1,0:T(4,128)S(1)}, f32[1,1,4,512]{3,2,1,0:T(4,128)S(1)}, u32[]{:S(2)}, u32[]{:S(2)}) collective-permute-start(f32[1,1,4,512]{3,2,1,0:T(4,128)S(1)} %get-tuple-element.163), channel_id=1, source_target_pairs={{0,1},{1,2},{2,3},{3,4},{4,5},{5,6},{6,7},{8,9},{9,10},{10,11},{11... | collective-permute-start | bytes 24584 | tf_op jit(solution)/shard_map/ppermute | solution.py:25
  34.0 16.4 %collective-permute-start = (f32[1,1,4,512]{3,2,1,0:T(4,128)S(1)}, f32[1,1,4,512]{3,2,1,0:T(4,128)S(1)}, u32[]{:S(2)}, u32[]{:S(2)}) collective-permute-start(f32[1,1,4,512]{3,2,1,0:T(4,128)S(1)} %get-tuple-element.164), channel_id=1, source_target_pairs={{1,0},{2,1},{3,2},{4,3},{5,4},{6,5},{7,6},{9,8},{10,9},{11,10},{12... | collective-permute-start | bytes 24584 | tf_op jit(solution)/shard_map/ppermute | solution.py:28
  39.4 54.3 %copy-start.56 = (f32[12,1]{0,1:T(1,128)}, f32[12,1]{0,1:T(1,128)S(1)}, u32[]{:S(2)}) copy-start(f32[12,1]{0,1:T(1,128)S(1)} %get-tuple-element.121) | copy-start | bytes 148
  39.5 54.2 %copy-start.51 = (f32[12,1]{0,1:T(1,128)}, f32[12,1]{0,1:T(1,128)S(1)}, u32[]{:S(2)}) copy-start(f32[12,1]{0,1:T(1,128)S(1)} %get-tuple-element.123) | copy-start | bytes 148
  39.5 54.2 %copy-start.58 = (f32[12,1]{0,1:T(1,128)}, f32[12,1]{0,1:T(1,128)S(1)}, u32[]{:S(2)}) copy-start(f32[12,1]{0,1:T(1,128)S(1)} %multiply_bitcast_fusion.1) | copy-start | bytes 148
  40.3 42.0 %copy-start.46 = (f32[3,12]{1,0:T(4,128)}, f32[3,12]{1,0:T(4,128)S(1)}, u32[]{:S(2)}) copy-start(f32[3,12]{1,0:T(4,128)S(1)} %broadcast_multiply_fusion.3) | copy-start | bytes 436
  44.2 35.4 %copy-start.38 = (f32[1,1,4,512]{3,2,1,0:T(4,128)}, f32[1,1,4,512]{3,2,1,0:T(4,128)S(1)}, u32[]{:S(2)}) copy-start(f32[1,1,4,512]{3,2,1,0:T(4,128)S(1)} %collective-permute-done.2) | copy-start | bytes 24580
  50.4 29.3 %copy-start.40 = (f32[1,1,4,512]{3,2,1,0:T(4,128)}, f32[1,1,4,512]{3,2,1,0:T(4,128)S(1)}, u32[]{:S(2)}) copy-start(f32[1,1,4,512]{3,2,1,0:T(4,128)S(1)} %collective-permute-done) | copy-start | bytes 24580
  50.4 28.9 %collective-permute-start.6 = (f32[1,14,1,512]{3,2,1,0:T(1,128)S(1)}, f32[1,14,1,512]{3,2,1,0:T(1,128)S(1)}, u32[]{:S(2)}, u32[]{:S(2)}) collective-permute-start(f32[1,14,1,512]{3,2,1,0:T(1,128)S(1)} %get-tuple-element.159), channel_id=1, source_target_pairs={{0,8},{8,16},{16,24},{24,32},{32,40},{40,48},{48,56},{56,64},{64,7... | collective-permute-start | bytes 86024 | tf_op jit(solution)/shard_map/ppermute | solution.py:25
  52.3 26.9 %collective-permute-start.4 = (f32[1,14,1,512]{3,2,1,0:T(1,128)S(1)}, f32[1,14,1,512]{3,2,1,0:T(1,128)S(1)}, u32[]{:S(2)}, u32[]{:S(2)}) collective-permute-start(f32[1,14,1,512]{3,2,1,0:T(1,128)S(1)} %get-tuple-element.160), channel_id=1, source_target_pairs={{8,0},{16,8},{24,16},{32,24},{40,32},{48,40},{56,48},{64,56},{72,6... | collective-permute-start | bytes 86024 | tf_op jit(solution)/shard_map/ppermute | solution.py:28
  64.7 17.6 %copy-start.34 = (f32[3,1,4,512]{3,2,1,0:T(4,128)}, f32[3,1,4,512]{3,2,1,0:T(4,128)S(1)}, u32[]{:S(2)}) copy-start(f32[3,1,4,512]{3,2,1,0:T(4,128)S(1)} %collective-permute-done.3) | copy-start | bytes 73732
  64.8 17.6 %copy-start.36 = (f32[3,1,4,512]{3,2,1,0:T(4,128)}, f32[3,1,4,512]{3,2,1,0:T(4,128)S(1)}, u32[]{:S(2)}) copy-start(f32[3,1,4,512]{3,2,1,0:T(4,128)S(1)} %collective-permute-done.1) | copy-start | bytes 73732
  65.0 15.3 %collective-permute-start.7 = (f32[3,14,1,512]{3,2,1,0:T(1,128)S(1)}, f32[3,14,1,512]{3,2,1,0:T(1,128)S(1)}, u32[]{:S(2)}, u32[]{:S(2)}) collective-permute-start(f32[3,14,1,512]{3,2,1,0:T(1,128)S(1)} %get-tuple-element.145), channel_id=1, source_target_pairs={{0,8},{8,16},{16,24},{24,32},{32,40},{40,48},{48,56},{56,64},{64,7... | collective-permute-start | bytes 258056 | tf_op jit(solution)/shard_map/ppermute | solution.py:25
  66.9 14.6 %collective-permute-start.5 = (f32[3,14,1,512]{3,2,1,0:T(1,128)S(1)}, f32[3,14,1,512]{3,2,1,0:T(1,128)S(1)}, u32[]{:S(2)}, u32[]{:S(2)}) collective-permute-start(f32[3,14,1,512]{3,2,1,0:T(1,128)S(1)} %get-tuple-element.146), channel_id=1, source_target_pairs={{8,0},{16,8},{24,16},{32,24},{40,32},{48,40},{56,48},{64,56},{72,6... | collective-permute-start | bytes 258056 | tf_op jit(solution)/shard_map/ppermute | solution.py:28
  80.2 2.2 copy-start.7
  80.2 147.3 %copy-start.1 = (f32[12,4,512]{2,1,0:T(4,128)}, f32[12,4,512]{2,1,0:T(4,128)S(1)}, u32[]{:S(2)}) copy-start(f32[12,4,512]{2,1,0:T(4,128)S(1)} %get-tuple-element.157) | copy-start | bytes 294916
  80.2 147.3 %copy-start.3 = (f32[12,4,512]{2,1,0:T(4,128)}, f32[12,4,512]{2,1,0:T(4,128)S(1)}, u32[]{:S(2)}) copy-start(f32[12,4,512]{2,1,0:T(4,128)S(1)} %get-tuple-element.158) | copy-start | bytes 294916
  80.2 147.3 %copy-start.5 = (f32[12,4,512]{2,1,0:T(4,128)}, f32[12,4,512]{2,1,0:T(4,128)S(1)}, u32[]{:S(2)}) copy-start(f32[12,4,512]{2,1,0:T(4,128)S(1)} %get-tuple-element.161) | copy-start | bytes 294916
  80.3 2.1 copy-start.16
  83.3 125.6 %collective-permute-start.9 = (f32[3,1,4,512]{3,2,1,0:T(4,128)S(1)}, f32[3,1,4,512]{3,2,1,0:T(4,128)S(1)}, u32[]{:S(2)}, u32[]{:S(2)}) collective-permute-start(f32[3,1,4,512]{3,2,1,0:T(4,128)S(1)} %get-tuple-element.151), channel_id=1, source_target_pairs={{0,1},{1,2},{2,3},{3,4},{4,5},{5,6},{6,7},{8,9},{9,10},{10,11},{11... | collective-permute-start | bytes 73736 | tf_op jit(solution)/shard_map/ppermute | solution.py:25
  91.8 117.2 %collective-permute-start.8 = (f32[3,1,4,512]{3,2,1,0:T(4,128)S(1)}, f32[3,1,4,512]{3,2,1,0:T(4,128)S(1)}, u32[]{:S(2)}, u32[]{:S(2)}) collective-permute-start(f32[3,1,4,512]{3,2,1,0:T(4,128)S(1)} %get-tuple-element.152), channel_id=1, source_target_pairs={{1,0},{2,1},{3,2},{4,3},{5,4},{6,5},{7,6},{9,8},{10,9},{11,10},{12... | collective-permute-start | bytes 73736 | tf_op jit(solution)/shard_map/ppermute | solution.py:28
  209.0 18.6 %copy-start.25 = (f32[3,1,4,512]{3,2,1,0:T(4,128)}, f32[3,1,4,512]{3,2,1,0:T(4,128)S(1)}, u32[]{:S(2)}) copy-start(f32[3,1,4,512]{3,2,1,0:T(4,128)S(1)} %collective-permute-done.9) | copy-start | bytes 73732
  209.6 14.5 %collective-permute-start.11 = (f32[3,14,1,512]{3,2,1,0:T(1,128)S(1)}, f32[3,14,1,512]{3,2,1,0:T(1,128)S(1)}, u32[]{:S(2)}, u32[]{:S(2)}) collective-permute-start(f32[3,14,1,512]{3,2,1,0:T(1,128)S(1)} %get-tuple-element.143), channel_id=1, source_target_pairs={{0,8},{8,16},{16,24},{24,32},{32,40},{40,48},{48,56},{56,64},{64,7... | collective-permute-start | bytes 258056 | tf_op jit(solution)/shard_map/ppermute | solution.py:25
  211.8 14.1 %collective-permute-start.10 = (f32[3,14,1,512]{3,2,1,0:T(1,128)S(1)}, f32[3,14,1,512]{3,2,1,0:T(1,128)S(1)}, u32[]{:S(2)}, u32[]{:S(2)}) collective-permute-start(f32[3,14,1,512]{3,2,1,0:T(1,128)S(1)} %get-tuple-element.144), channel_id=1, source_target_pairs={{8,0},{16,8},{24,16},{32,24},{40,32},{48,40},{56,48},{64,56},{72,6... | collective-permute-start | bytes 258056 | tf_op jit(solution)/shard_map/ppermute | solution.py:28
  223.9 3.7 copy-start.49
  223.9 3.7 copy-start.8
  223.9 3.7 copy-start.28
  223.9 3.7 copy-start.44
  224.1 3.5 copy-start.12
  225.9 1.6 copy-start.14
  225.9 1.7 copy-start.47
  729.5 35.5 %copy-start.53 = (f32[3,12]{1,0:T(4,128)S(1)}, f32[3,12]{1,0:T(4,128)}, u32[]{:S(2)}) copy-start(f32[3,12]{1,0:T(4,128)} %param.19) | copy-start | bytes 436
  729.5 35.5 %copy-start.54 = (f32[3,12]{1,0:T(4,128)S(1)}, f32[3,12]{1,0:T(4,128)}, u32[]{:S(2)}) copy-start(f32[3,12]{1,0:T(4,128)} %param.18) | copy-start | bytes 436
  909.4 14.7 %collective-permute-start.13 = (f32[3,1,4,512]{3,2,1,0:T(4,128)S(1)}, f32[3,1,4,512]{3,2,1,0:T(4,128)S(1)}, u32[]{:S(2)}, u32[]{:S(2)}) collective-permute-start(f32[3,1,4,512]{3,2,1,0:T(4,128)S(1)} %get-tuple-element.149), channel_id=1, source_target_pairs={{0,1},{1,2},{2,3},{3,4},{4,5},{5,6},{6,7},{8,9},{9,10},{10,11},{11... | collective-permute-start | bytes 73736 | tf_op jit(solution)/shard_map/ppermute | solution.py:25
  922.2 16.5 %collective-permute-start.12 = (f32[3,1,4,512]{3,2,1,0:T(4,128)S(1)}, f32[3,1,4,512]{3,2,1,0:T(4,128)S(1)}, u32[]{:S(2)}, u32[]{:S(2)}) collective-permute-start(f32[3,1,4,512]{3,2,1,0:T(4,128)S(1)} %get-tuple-element.150), channel_id=1, source_target_pairs={{1,0},{2,1},{3,2},{4,3},{5,4},{6,5},{7,6},{9,8},{10,9},{11,10},{12... | collective-permute-start | bytes 73736 | tf_op jit(solution)/shard_map/ppermute | solution.py:28
  924.1 15.4 %copy-start.21 = (f32[3,1,4,512]{3,2,1,0:T(4,128)}, f32[3,1,4,512]{3,2,1,0:T(4,128)S(1)}, u32[]{:S(2)}) copy-start(f32[3,1,4,512]{3,2,1,0:T(4,128)S(1)} %collective-permute-done.13) | copy-start | bytes 73732
  939.5 225.9 %collective-permute-start.15 = (f32[3,14,1,512]{3,2,1,0:T(1,128)}, f32[3,14,1,512]{3,2,1,0:T(1,128)}, u32[]{:S(2)}, u32[]{:S(2)}) collective-permute-start(f32[3,14,1,512]{3,2,1,0:T(1,128)} %get-tuple-element.141), channel_id=1, source_target_pairs={{0,8},{8,16},{16,24},{24,32},{32,40},{40,48},{48,56},{56,64},{64,7... | collective-permute-start | bytes 258056 | tf_op jit(solution)/shard_map/ppermute | solution.py:25
  941.5 224.0 %collective-permute-start.14 = (f32[3,14,1,512]{3,2,1,0:T(1,128)}, f32[3,14,1,512]{3,2,1,0:T(1,128)}, u32[]{:S(2)}, u32[]{:S(2)}) collective-permute-start(f32[3,14,1,512]{3,2,1,0:T(1,128)} %get-tuple-element.142), channel_id=1, source_target_pairs={{8,0},{16,8},{24,16},{32,24},{40,32},{48,40},{56,48},{64,56},{72,6... | collective-permute-start | bytes 258056 | tf_op jit(solution)/shard_map/ppermute | solution.py:28
  1165.3 2.0 copy-start.2
  1165.3 2.0 copy-start.4
  1165.4 2.0 copy-start.6
  1165.4 2.0 copy-start.9
  1165.4 2.0 copy-start.22
  1165.4 2.0 copy-start.24
  1165.4 2.0 copy-start.50
  1169.1 5.9 copy-start.26
  1169.1 5.9 copy-start.29
  1169.1 6.8 collective-permute-start.17
  1171.1 16.5 %collective-permute-start.16 = (f32[3,1,4,512]{3,2,1,0:T(4,128)S(1)}, f32[3,1,4,512]{3,2,1,0:T(4,128)S(1)}, u32[]{:S(2)}, u32[]{:S(2)}) collective-permute-start(f32[3,1,4,512]{3,2,1,0:T(4,128)S(1)} %get-tuple-element.148), channel_id=1, source_target_pairs={{1,0},{2,1},{3,2},{4,3},{5,4},{6,5},{7,6},{9,8},{10,9},{11,10},{12... | collective-permute-start | bytes 73736 | tf_op jit(solution)/shard_map/ppermute | solution.py:28
  1175.9 26.3 %copy-start.13 = (f32[3,14,1,512]{3,2,1,0:T(1,128)S(1)}, f32[3,14,1,512]{3,2,1,0:T(1,128)}, u32[]{:S(2)}) copy-start(f32[3,14,1,512]{3,2,1,0:T(1,128)} %copy-done.12) | copy-start | bytes 258052
  1175.9 26.3 %copy-start.15 = (f32[3,14,1,512]{3,2,1,0:T(1,128)S(1)}, f32[3,14,1,512]{3,2,1,0:T(1,128)}, u32[]{:S(2)}) copy-start(f32[3,14,1,512]{3,2,1,0:T(1,128)} %copy-done.14) | copy-start | bytes 258052
  1187.7 16.2 %collective-permute-start.19 = (f32[3,14,1,512]{3,2,1,0:T(1,128)S(1)}, f32[3,14,1,512]{3,2,1,0:T(1,128)S(1)}, u32[]{:S(2)}, u32[]{:S(2)}) collective-permute-start(f32[3,14,1,512]{3,2,1,0:T(1,128)S(1)} %get-tuple-element.139), channel_id=1, source_target_pairs={{0,8},{8,16},{16,24},{24,32},{32,40},{40,48},{48,56},{56,64},{64,7... | collective-permute-start | bytes 258056 | tf_op jit(solution)/shard_map/ppermute | solution.py:25
  1189.7 14.6 %copy-start.17 = (f32[3,14,1,512]{3,2,1,0:T(1,128)S(1)}, f32[3,14,1,512]{3,2,1,0:T(1,128)}, u32[]{:S(2)}) copy-start(f32[3,14,1,512]{3,2,1,0:T(1,128)} %copy-done.16) | copy-start | bytes 258052
  1189.7 14.6 %copy-start.19 = (f32[3,14,1,512]{3,2,1,0:T(1,128)S(1)}, f32[3,14,1,512]{3,2,1,0:T(1,128)}, u32[]{:S(2)}) copy-start(f32[3,14,1,512]{3,2,1,0:T(1,128)} %copy-done.18) | copy-start | bytes 258052
  1189.7 14.6 %copy-start.37 = (f32[3,1,4,512]{3,2,1,0:T(4,128)S(1)}, f32[3,1,4,512]{3,2,1,0:T(4,128)}, u32[]{:S(2)}) copy-start(f32[3,1,4,512]{3,2,1,0:T(4,128)} %copy-done.36) | copy-start | bytes 73732
  1189.7 14.6 %collective-permute-start.18 = (f32[3,14,1,512]{3,2,1,0:T(1,128)S(1)}, f32[3,14,1,512]{3,2,1,0:T(1,128)S(1)}, u32[]{:S(2)}, u32[]{:S(2)}) collective-permute-start(f32[3,14,1,512]{3,2,1,0:T(1,128)S(1)} %get-tuple-element.140), channel_id=1, source_target_pairs={{8,0},{16,8},{24,16},{32,24},{40,32},{48,40},{56,48},{64,56},{72,6... | collective-permute-start | bytes 258056 | tf_op jit(solution)/shard_map/ppermute | solution.py:28
  1206.0 0.9 copy-start.11
  1206.0 1.0 copy-start.42
  (17 other events, 12.4 us)
where the time goes:
time: 1210 us
  blocking collectives  961 us (79%)
  starting transfers between devices  137 us (11%)
  waiting for transfers between devices  36.1 us (3%)
  matrix products  32.3 us (3%)
  other arithmetic  19.4 us (2%)
  local copies, waits for them, and re-layouts  16 us (1%)
    unnamed x1, blocking collectives  423 us
    psum x1, blocking collectives, body(): lax.psum(jnp.sum(weighted * weighted), 'lon')  211 us
    all_gather x1, blocking collectives, body(): piece = lax.all_gather(packet, 'lon', axis=0, tiled=True)  113 us
    all_gather x1, blocking collectives, body(): all_feats = lax.all_gather(own_feats, 'lon', axis=0, tiled=True)  113 us
    ppermute x10, starting transfers between devices, extended(): lax.ppermute(lax.slice_in_dim(block, 0, width, axis=dim), axis, backward)  73.2 us
    psum x1, blocking collectives, body(): whole_column = lax.psum(column, 'rad')  65.8 us
    ppermute x10, starting transfers between devices, extended(): lax.ppermute(lax.slice_in_dim(block, block.shape[dim] - width, None, axis...  63.6 us
    ppermute x10, waiting for transfers between devices, extended(): lax.ppermute(lax.slice_in_dim(block, 0, width, axis=dim), axis, backward)  35.9 us
  transfers between devices with their start and end apart: 20, of which 7 were waited for; matrix products, arithmetic and copies ran while one was open for 1% of the time, Pallas kernels for 0%

commit v1 on v0

v1 whole, which is shorter than its diff:
```python
import functools
import math

import jax
import jax.numpy as jnp
from jax import lax
from jax.experimental import pallas as pl
from jax.experimental.pallas import tpu as pltpu
from jax.sharding import PartitionSpec as P

MESH = pl.DeviceIdType.MESH
NR, NLON, NLAT = 96, 256, 512
ROWS = 12
COLS = 4
SCALE = 1.0 / math.sqrt(NLON * NLAT)
WAVE = [0.5 * (-1) ** k * (2.0 * math.pi) ** (2 * k + 1) / math.factorial(2 * k + 1) for k in range(6)]


def place():
    lon, rad = lax.axis_index("lon"), lax.axis_index("rad")
    return lon // 16, (rad // 4) * 8 + (lon // 2) % 8, lon % 2, rad % 4


def device(y, z, c, x):
    return (y * 16 + (z % 8) * 2 + c, (z // 8) * 4 + x)


def z_peer(i):
    y, z, c, x = place()
    z2 = (z + i) % 16
    return device(y, z2, c, x), z2


def plane_peer(i):
    y, z, c, x = place()
    x2, y2, c2 = (x + i % 4) % 4, (y + (i // 4) % 4) % 4, (c + i // 16) % 2
    return device(y2, z, c2, x2), x2, y2 * 2 + c2


def block_peer(i):
    y, z, c, x = place()
    y2, c2 = (y + i % 4) % 4, (c + i // 4) % 2
    return device(y2, z, c2, x), y2 * 2 + c2


def x_peer(i):
    y, z, c, x = place()
    x2 = (x + i) % 4
    return device(y, z, c, x2), x2


def repeat(first, last, step):
    def one(i, carry):
        step(i)
        return carry

    lax.fori_loop(first, last, one, 0)


def send(src, dst, ssem, rsem, target):
    pltpu.make_async_remote_copy(
        src_ref=src, dst_ref=dst, send_sem=ssem, recv_sem=rsem, device_id=target, device_id_type=MESH
    ).start()


def await_bytes(ref, sem):
    pltpu.make_async_copy(ref, ref, sem).wait()


def iota(shape, dim):
    return lax.broadcasted_iota(jnp.int32, shape, dim)


def next_lat(v):
    return pltpu.roll(v, NLAT - 1, v.ndim - 1)


def last_lat(v):
    return pltpu.roll(v, 1, v.ndim - 1)


def next_row(v):
    return pltpu.roll(v, 15, 0)


def last_row(v):
    return pltpu.roll(v, 1, 0)


def blocks_to_lanes(blocks):
    lane = iota((8, 128), 1)
    tiles = []
    for t in range(6):
        b = (128 * t) // 96
        first, second = 96 * b - 128 * t, 96 * (b + 1) - 128 * t
        low = pltpu.roll(blocks[b], first % 128, 1) if first % 128 else blocks[b]
        high = pltpu.roll(blocks[b + 1], second % 128, 1)
        tiles.append(jnp.where(lane < second, low, high))
    return tiles


def lanes_to_blocks(tiles):
    lane = iota((8, 128), 1)
    blocks = []
    for b in range(8):
        t, offset = (96 * b) // 128, (96 * b) % 128
        block = pltpu.roll(tiles[t], 128 - offset, 1) if offset else tiles[t]
        if offset > 32:
            block = jnp.where(lane < 128 - offset, block, pltpu.roll(tiles[t + 1], 128 - offset, 1))
        blocks.append(jnp.where(lane < 96, block, 0.0))
    return blocks


def split(v):
    high = v.astype(jnp.bfloat16)
    return high, (v - high.astype(jnp.float32)).astype(jnp.bfloat16)


def kernel(
    lv_ref, u_ref, ice_ref, steps_ref, cells_ref, observed_ref, weight_ref,
    grad_ref, misfit_ref,
    X, E, S1, QA, QO, QR, radS, radR, lvS, lvR,
    packet, gathered, block, sites, SB, RB, KH, KL,
    PB, C1R, C2S, C2R, C3S, C3R, SD, DR, ssem, rsem,
):
    lon, rad = lax.axis_index("lon"), lax.axis_index("rad")
    y, z, c, x = place()
    own_block = y * 2 + c
    right, left = ((lon + 1) % 64, rad), ((lon + 63) % 64, rad)
    above, below = (lon, (rad + 1) % 8), (lon, (rad + 7) % 8)

    barrier = pltpu.get_barrier_semaphore()

    def greet(target):
        pl.semaphore_signal(barrier, 1, device_id=target, device_id_type=MESH)

    for target in (right, left, above, below):
        greet(target)
    repeat(1, 16, lambda i: greet(z_peer(i)[0]))
    repeat(1, 32, lambda i: greet(plane_peer(i)[0]))

    for f in range(4):
        for l in range(COLS):
            source = lv_ref[:, l, :] if f == 0 else u_ref[f - 1, :, l, :]
            X[f, l + 2, 0:ROWS, :] = source
            X[f, l + 2, ROWS:16, :] = jnp.zeros((16 - ROWS, NLAT), jnp.float32)
            radS[0, f * 4 + l : f * 4 + l + 1, :] = source[11:12, :]
            radS[1, f * 4 + l : f * 4 + l + 1, :] = source[0:1, :]
    packet[...] = jnp.zeros((8, 128), jnp.float32)
    packet[0:1, 0:12] = cells_ref[...].astype(jnp.float32)
    packet[1:4, 0:12] = observed_ref[...]
    packet[4:7, 0:12] = weight_ref[...]
    gathered[z % 8] = packet[...]

    pl.semaphore_wait(barrier, 50)

    send(radS.at[0], radR.at[0], ssem.at[0], rsem.at[0], above)
    send(radS.at[1], radR.at[1], ssem.at[1], rsem.at[1], below)
    send(X.at[:, 5], X.at[:, 1], ssem.at[2], rsem.at[2], right)
    send(X.at[:, 2], X.at[:, 6], ssem.at[3], rsem.at[3], left)

    def send_record(i):
        target, unused = z_peer((i + 12) % 16)
        send(packet, gathered.at[z % 8], ssem.at[4], rsem.at[4], target)

    repeat(0, 4, send_record)
    repeat(5, 8, send_record)

    row = iota((16, NLAT), 0)
    layer = jnp.where(row >= 14, row - 16, row)
    depth = (layer + rad * ROWS).astype(jnp.float32)
    wr = jnp.exp(4.0 * (depth - (NR - 1)) / NR)
    wr_next = jnp.exp(4.0 * (depth + 1.0 - (NR - 1)) / NR)
    own_row = row < ROWS
    wr_own = jnp.where(own_row, wr, 0.0)
    deep = layer + rad * ROWS
    face_ok = (row != 13) & (deep >= 0) & (deep < NR - 1)
    not_last = iota((16, NLAT), 1) < NLAT - 1
    is_top = jnp.where(rad == 7, 1.0, 0.0)

    await_bytes(gathered.at[pl.ds(0, 7)], rsem.at[4])
    record = gathered[0]
    for slot in range(1, 8):
        record = record + pltpu.roll(gathered[slot], 12 * slot, 1)
    block[...] = record
    sites[own_block] = record

    def send_block(i):
        target, unused = block_peer(i)
        send(block, sites.at[own_block], ssem.at[5], rsem.at[5], target)

    repeat(1, 8, send_block)

    await_bytes(radR.at[0], rsem.at[0])
    await_bytes(radR.at[1], rsem.at[1])
    await_bytes(X.at[:, 1], rsem.at[2])
    await_bytes(X.at[:, 6], rsem.at[3])
    await_bytes(X.at[:, 5], ssem.at[2])
    await_bytes(X.at[:, 2], ssem.at[3])
    for f in range(4):
        for l in range(COLS):
            X[f, l + 2, 15:16, :] = radR[0, f * 4 + l : f * 4 + l + 1, :]
            X[f, l + 2, 12:13, :] = radR[1, f * 4 + l : f * 4 + l + 1, :]

    def edge_lat(e):
        return jnp.where(not_last, 0.1 / (e + next_lat(e)), 0.0)

    def edge_rad(e):
        return jnp.where(face_ok, 0.1 / (e + next_row(e)), 0.0)

    for p in range(1, 7):
        E[p] = jnp.exp(X[0, p])
    for p in range(2, 6):
        QA[p] = edge_lat(E[p])
        QR[p] = edge_rad(E[p])
    for p in range(1, 6):
        QO[p] = 0.1 / (E[p] + E[p + 1])
    load_1, load_2 = ice_ref[steps_ref[0]], ice_ref[steps_ref[1]]
    for f in range(3):
        for p in range(2, 6):
            u = X[f + 1, p]
            flux = QA[p] * (next_lat(u) - u)
            rise = QR[p] * (next_row(u) - u)
            total = u + (flux - last_lat(flux)) + (rise - last_row(rise))
            total = total + QO[p] * (X[f + 1, p + 1] - u) + QO[p - 1] * (X[f + 1, p - 1] - u)
            if f == 0:
                pressed = jnp.broadcast_to(load_1[p - 2 : p - 1, :], (16, NLAT)) * is_top
                total = total - jnp.where(row == ROWS - 1, pressed, 0.0)
            S1[f, p] = total

    columns = []
    for f in range(3):
        columns.append([jnp.zeros((1, NLAT), jnp.float32) for unused in range(8)])

    def column_sum(v):
        return jnp.sum(v, axis=0, keepdims=True)

    for p in range(2, 6):
        slope = QR[p] * (wr_next - wr)
        factor = jnp.where(own_row, wr + slope - last_row(slope), 0.0)
        along = wr_own * QA[p]
        for f in range(3):
            s = S1[f, p]
            flux = column_sum(along * (next_lat(s) - s))
            columns[f][p] = columns[f][p] + column_sum(factor * s) + (flux - last_lat(flux))
    for p in range(1, 6):
        across = wr_own * QO[p]
        for f in range(3):
            if p == 1:
                flow = column_sum(across * S1[f, 2])
            elif p == 5:
                flow = -column_sum(across * S1[f, 5])
            else:
                flow = column_sum(across * (S1[f, p + 1] - S1[f, p]))
            columns[f][p] = columns[f][p] + flow
            columns[f][p + 1] = columns[f][p + 1] - flow
    for p in range(2, 6):
        columns[0][p] = columns[0][p] - load_2[p - 2 : p - 1, :] * is_top
    for f in range(3):
        for p in range(8):
            for band in range(4):
                SB[band, f * 8 + p : f * 8 + p + 1, :] = columns[f][p][:, band * 128 : band * 128 + 128]
    RB[x] = SB[x]

    def send_band(i):
        target, x2 = x_peer(i)
        send(SB.at[x2], RB.at[x], ssem.at[6], rsem.at[6], target)

    repeat(1, 4, send_band)

    for f in range(3):
        for l in range(COLS):
            radS[2, f * 4 + l : f * 4 + l + 1, :] = S1[f, l + 2, 11:12, :]
            radS[3, f * 4 + l : f * 4 + l + 1, :] = S1[f, l + 2, 0:1, :]
    for l in range(COLS):
        radS[2, 12 + l : 13 + l, :] = X[0, l + 2, 10:11, :]
        radS[3, 12 + l : 13 + l, :] = X[0, l + 2, 1:2, :]
    lvS[0] = jnp.where(own_row, X[0, 4], X[0, 5])
    lvS[1] = jnp.where(own_row, X[0, 3], X[0, 2])
    send(radS.at[2], radR.at[2], ssem.at[7], rsem.at[7], above)
    send(radS.at[3], radR.at[3], ssem.at[8], rsem.at[8], below)
    send(S1.at[:, 5], S1.at[:, 1], ssem.at[9], rsem.at[9], right)
    send(S1.at[:, 2], S1.at[:, 6], ssem.at[10], rsem.at[10], left)
    send(lvS.at[0], lvR.at[0], ssem.at[11], rsem.at[11], right)
    send(lvS.at[1], lvR.at[1], ssem.at[12], rsem.at[12], left)

    await_bytes(sites.at[pl.ds(0, 7)], rsem.at[5])
    tiles = blocks_to_lanes([sites[b] for b in range(8)])
    theta = (iota((128, 128), 0) + x * 128).astype(jnp.float32)
    theta = math.pi * (theta + 0.5) / NLAT
    cell_cos, cell_sin = jnp.cos(theta), jnp.sin(theta)
    plane_lon = (iota((8, 128), 0) + (lon * COLS - 2)).astype(jnp.float32)
    for t in range(6):
        cell = jnp.broadcast_to(tiles[t][0:1, :], (8, 128))
        site_lon = jnp.floor(cell * (1.0 / NLAT))
        site_theta = math.pi * (cell - NLAT * site_lon + 0.5) / NLAT
        up = jnp.cos(site_theta)
        side = jnp.sin(site_theta) * jnp.cos(2.0 * math.pi * (site_lon - plane_lon) / NLON)
        for p in range(8):
            cosine = cell_cos * up[0:1, :] + cell_sin * side[p : p + 1, :]
            chord = 2.0 - 2.0 * cosine
            turns = chord * (40.0 / (2.0 * math.pi))
            turns = 0.25 - jnp.abs(turns - jnp.round(turns))
            squared = turns * turns
            wave = jnp.full_like(squared, WAVE[5])
            for k in range(4, -1, -1):
                wave = wave * squared + WAVE[k]
            value = 1.0 / (1.0 + chord * 10.0) + wave * turns
            high, low = split(value)
            KH[p * 128 : p * 128 + 128, t * 128 : t * 128 + 128] = high
            KL[p * 128 : p * 128 + 128, t * 128 : t * 128 + 128] = low

    await_bytes(RB.at[pl.ds(0, 3)], rsem.at[6])
    band = (RB[0] + RB[1]) + (RB[2] + RB[3])
    place_of = iota((24, 128), 0) % 8
    wide = jnp.concatenate([jnp.where(place_of == p, band, 0.0) for p in range(8)], axis=1)
    high, low = split(wide)
    dot = functools.partial(jnp.dot, preferred_element_type=jnp.float32)
    parts = dot(high, KH[...]) + dot(high, KL[...]) + dot(low, KH[...])
    row8 = iota((8, 6 * 128), 0)
    pred = jnp.zeros((8, 6 * 128), jnp.float32)
    for f in range(3):
        summed = jnp.sum(parts[f * 8 : f * 8 + 8, :], axis=0, keepdims=True) * SCALE
        pred = jnp.where(row8 == f, jnp.broadcast_to(summed, pred.shape), pred)
    pieces = lanes_to_blocks([pred[:, t * 128 : t * 128 + 128] for t in range(6)])
    for b in range(8):
        PB[b] = pieces[b]
    C1R[x * 8 + own_block] = PB[own_block]

    def send_piece(i):
        target, unused, b2 = plane_peer(i)
        send(PB.at[b2], C1R.at[x * 8 + own_block], ssem.at[13], rsem.at[13], target)

    repeat(1, 32, send_piece)
    await_bytes(C1R.at[pl.ds(0, 31)], rsem.at[13])
    summed = jnp.sum(C1R[...], axis=0)
    C2S[...] = summed
    C2R[z] = summed

    def send_sum(i):
        target, unused = z_peer(i)
        send(C2S, C2R.at[z], ssem.at[14], rsem.at[14], target)

    repeat(1, 16, send_sum)

    await_bytes(radR.at[2], rsem.at[7])
    await_bytes(radR.at[3], rsem.at[8])
    await_bytes(S1.at[:, 1], rsem.at[9])
    await_bytes(S1.at[:, 6], rsem.at[10])
    await_bytes(lvR.at[0], rsem.at[11])
    await_bytes(lvR.at[1], rsem.at[12])
    await_bytes(S1.at[:, 5], ssem.at[9])
    await_bytes(S1.at[:, 2], ssem.at[10])
    for f in range(3):
        for l in range(COLS):
            S1[f, l + 2, 15:16, :] = radR[2, f * 4 + l : f * 4 + l + 1, :]
            S1[f, l + 2, 12:13, :] = radR[3, f * 4 + l : f * 4 + l + 1, :]
    for l in range(COLS):
        X[0, l + 2, 14:15, :] = radR[2, 12 + l : 13 + l, :]
        X[0, l + 2, 13:14, :] = radR[3, 12 + l : 13 + l, :]
    for side, far, near in ((0, 0, 1), (1, 7, 6)):
        X[0, far] = lvR[side]
        X[0, near] = jnp.where(own_row, X[0, near], lvR[side])
    for p in range(8):
        E[p] = jnp.exp(X[0, p])
    for p in range(1, 7):
        QA[p] = edge_lat(E[p])
        QR[p] = edge_rad(E[p])
    for p in range(7):
        QO[p] = 0.1 / (E[p] + E[p + 1])

    await_bytes(C2R.at[pl.ds(0, 15)], rsem.at[14])
    predicted = jnp.sum(C2R[...], axis=0)
    record = block[...]
    row_of, lane_of = iota((8, 128), 0), iota((8, 128), 1)
    entry = (row_of < 3) & (lane_of < 96)
    weight = jnp.where(entry, pltpu.roll(record, 4, 0), 0.0)
    weighted = weight * (predicted - pltpu.roll(record, 7, 0))
    squares = jnp.broadcast_to(jnp.sum(weighted * weighted, axis=0, keepdims=True), (8, 128))
    pulled = jnp.where(row_of == 3, squares, weight * weighted)
    C3S[...] = pulled
    C3R[own_block] = pulled

    def send_pulled(i):
        target, unused = block_peer(i)
        send(C3S, C3R.at[own_block], ssem.at[15], rsem.at[15], target)

    repeat(1, 8, send_pulled)
    await_bytes(C3R.at[pl.ds(0, 7)], rsem.at[15])
    pulls = [C3R[b] for b in range(8)]
    total = pulls[0]
    for b in range(1, 8):
        total = total + pulls[b]
    misfit_ref[0] = jnp.sum(total[3:4, :]) / (3.0 * 768.0)
    pull = jnp.concatenate(blocks_to_lanes(pulls), axis=1)
    high, low = split(pull)
    both = jnp.concatenate([high, low], axis=0)

    def against(lhs, rhs):
        return lax.dot_general(lhs, rhs, (((1,), (1,)), ((), ())), preferred_element_type=jnp.float32)

    first = against(both, KH[...])
    adjoint = (first[0:8] + first[8:16] + against(both, KL[...])[0:8]) * SCALE
    SD[...] = adjoint
    DR[x] = adjoint

    def send_adjoint(i):
        target, unused = x_peer(i)
        send(SD, DR.at[x], ssem.at[16], rsem.at[16], target)

    repeat(1, 4, send_adjoint)
    await_bytes(DR.at[pl.ds(0, 3)], rsem.at[16])

    faces_a = [jnp.zeros((16, NLAT), jnp.float32) for unused in range(8)]
    faces_r = [jnp.zeros((16, NLAT), jnp.float32) for unused in range(8)]
    faces_o = [jnp.zeros((16, NLAT), jnp.float32) for unused in range(8)]
    for f in range(3):
        a2 = []
        for p in range(8):
            surface = jnp.concatenate(
                [DR[band, f : f + 1, p * 128 : p * 128 + 128] for band in range(4)], axis=1
            )
            a2.append(wr * jnp.broadcast_to(surface, (16, NLAT)))
        a1 = [None] * 8
        for p in range(1, 7):
            flux = QA[p] * (next_lat(a2[p]) - a2[p])
            rise = QR[p] * (next_row(a2[p]) - a2[p])
            a1[p] = (
                a2[p] + (flux - last_lat(flux)) + (rise - last_row(rise))
                + QO[p] * (a2[p + 1] - a2[p]) + QO[p - 1] * (a2[p - 1] - a2[p])
            )
        for p in range(1, 6):
            u, s = X[f + 1, p], S1[f, p]
            faces_o[p] = (
                faces_o[p]
                + (X[f + 1, p + 1] - u) * (a1[p + 1] - a1[p])
                + (S1[f, p + 1] - s) * (a2[p + 1] - a2[p])
            )
            if p > 1:
                faces_a[p] = (
                    faces_a[p]
                    + (next_lat(u) - u) * (next_lat(a1[p]) - a1[p])
                    + (next_lat(s) - s) * (next_lat(a2[p]) - a2[p])
                )
                faces_r[p] = (
                    faces_r[p]
                    + (next_row(u) - u) * (next_row(a1[p]) - a1[p])
                    + (next_row(s) - s) * (next_row(a2[p]) - a2[p])
                )
    for p in range(1, 6):
        faces_o[p] = QO[p] * QO[p] * faces_o[p]
    for p in range(2, 6):
        along = QA[p] * QA[p] * faces_a[p]
        upward = QR[p] * QR[p] * faces_r[p]
        whole = (along + last_lat(along)) + (upward + last_row(upward)) + (faces_o[p] + faces_o[p - 1])
        result = 10.0 * E[p] * whole + 0.1 * X[0, p]
        grad_ref[:, p - 2, :] = result[0:ROWS, :]

    for k, ref in ((0, radS.at[0]), (1, radS.at[1]), (4, gathered.at[pl.ds(0, 7)]), (5, sites.at[pl.ds(0, 7)]), (6, RB.at[pl.ds(0, 3)]),
                   (7, radS.at[2]), (8, radS.at[3]), (11, lvS.at[0]),
                   (12, lvS.at[1]), (13, C1R.at[pl.ds(0, 31)]), (14, C2R.at[pl.ds(0, 15)]),
                   (15, C3R.at[pl.ds(0, 7)]), (16, DR.at[pl.ds(0, 3)])):
        await_bytes(ref, ssem.at[k])


def body(logvisc, momentum, displacement, ice_history, load_steps, site_cells, observed, site_weight):
    f32 = jnp.float32
    vmem = pl.BlockSpec(memory_space=pltpu.VMEM)
    smem = pl.BlockSpec(memory_space=pltpu.SMEM)
    gradient, misfit = pl.pallas_call(
        kernel,
        out_shape=(
            jax.ShapeDtypeStruct((ROWS, COLS, NLAT), f32),
            jax.ShapeDtypeStruct((1,), f32),
        ),
        in_specs=[vmem, vmem, vmem, smem, vmem, vmem, vmem],
        out_specs=(vmem, smem),
        scratch_shapes=[
            pltpu.VMEM((4, 8, 16, NLAT), f32),
            pltpu.VMEM((8, 16, NLAT), f32),
            pltpu.VMEM((3, 8, 16, NLAT), f32),
            pltpu.VMEM((8, 16, NLAT), f32),
            pltpu.VMEM((8, 16, NLAT), f32),
            pltpu.VMEM((8, 16, NLAT), f32),
            pltpu.VMEM((4, 16, NLAT), f32),
            pltpu.VMEM((4, 16, NLAT), f32),
            pltpu.VMEM((2, 16, NLAT), f32),
            pltpu.VMEM((2, 16, NLAT), f32),
            pltpu.VMEM((8, 128), f32),
            pltpu.VMEM((8, 8, 128), f32),
            pltpu.VMEM((8, 128), f32),
            pltpu.VMEM((8, 8, 128), f32),
            pltpu.VMEM((4, 24, 128), f32),
            pltpu.VMEM((4, 24, 128), f32),
            pltpu.VMEM((1024, 768), jnp.bfloat16),
            pltpu.VMEM((1024, 768), jnp.bfloat16),
            pltpu.VMEM((8, 8, 128), f32),
            pltpu.VMEM((32, 8, 128), f32),
            pltpu.VMEM((8, 128), f32),
            pltpu.VMEM((16, 8, 128), f32),
            pltpu.VMEM((8, 128), f32),
            pltpu.VMEM((8, 8, 128), f32),
            pltpu.VMEM((8, 1024), f32),
            pltpu.VMEM((4, 8, 1024), f32),
            pltpu.SemaphoreType.DMA((17,)),
            pltpu.SemaphoreType.DMA((17,)),
        ],
        compiler_params=pltpu.CompilerParams(
            collective_id=0, has_side_effects=True, vmem_limit_bytes=48 * 1024 * 1024
        ),
    )(logvisc, displacement, ice_history, load_steps, site_cells.reshape(1, 12), observed, site_weight)
    half_momentum = momentum - 0.5 * gradient
    return logvisc + half_momentum, half_momentum, misfit


def solution(mesh):
    return jax.shard_map(
        body,
        mesh=mesh,
        in_specs=(
            P("rad", "lon", None),
            P("rad", "lon", None),
            P(None, "rad", "lon", None),
            P(None, "lon", None),
            P(),
            P("lon"),
            P(None, "lon"),
            P(None, "lon"),
        ),
        out_specs=(P("rad", "lon", None), P("rad", "lon", None), P()),
        check_vma=False,
    )
```

time: 1210 us -> 66.9 us (0.06)
  the two profiles are of different devices: /device:TPU:6 before, /device:TPU:1 now
where the time goes in v1:
time: 66.9 us; the launch traced here: 66.6 us
  Pallas kernels  58.7 us (88%)
  local copies, waits for them, and re-layouts  4.71 us (7%)
  between operations  2.43 us (4%)
  other arithmetic  0.73 us (1%)
    pallas_call x1, Pallas kernels, body(): pl.pallas_call(kernel, out_shape=(jax.ShapeDtypeStruct((ROWS, COLS, NLAT)...  58.7 us
    unnamed x16, local copies, waits for them, and re-layouts  4.71 us

profile of v1, /device:TPU:1, one launch (start us, length us, event | category | flops | bytes accessed | tf_op | source)
XLA Modules:
  0.0 66.6 jit_solution(16899556934883508008)
XLA Ops:
  0.6 0.0 copy-start.6
  0.6 0.0 copy-start.5
  0.7 0.6 copy-done.6
  1.3 0.0 copy-done.5
  1.3 0.0 copy-start
  1.3 0.9 %copy-done = f32[12,4,512]{2,1,0:T(4,128)S(1)} copy-done((f32[12,4,512]{2,1,0:T(4,128)S(1)}, f32[12,4,512]{2,1,0:T(4,128)}, u32[]{:S(2)}) %copy-start) | copy-done | bytes 98328
  2.2 0.0 copy-start.1
  2.2 1.0 %copy-done.1 = f32[3,12,4,512]{3,2,1,0:T(4,128)S(1)} copy-done((f32[3,12,4,512]{3,2,1,0:T(4,128)S(1)}, f32[3,12,4,512]{3,2,1,0:T(4,128)}, u32[]{:S(2)}) %copy-start.1) | copy-done | bytes 294936
  3.2 0.0 copy-start.2
  3.2 0.8 %copy-done.2 = f32[8,4,512]{2,1,0:T(4,128)S(1)} copy-done((f32[8,4,512]{2,1,0:T(4,128)S(1)}, f32[8,4,512]{2,1,0:T(4,128)}, u32[]{:S(2)}) %copy-start.2) | copy-done | bytes 65560
  4.0 0.0 copy-start.3
  4.0 0.7 %copy-done.3 = f32[3,12]{1,0:T(4,128)S(1)} copy-done((f32[3,12]{1,0:T(4,128)S(1)}, f32[3,12]{1,0:T(4,128)}, u32[]{:S(2)}) %copy-start.3) | copy-done | bytes 168
  4.7 0.0 copy-start.4
  4.7 0.7 %copy-done.4 = f32[3,12]{1,0:T(4,128)S(1)} copy-done((f32[3,12]{1,0:T(4,128)S(1)}, f32[3,12]{1,0:T(4,128)}, u32[]{:S(2)}) %copy-start.4) | copy-done | bytes 168
  5.4 0.0 copy-start.7
  5.4 58.7 %shard_map.103 = (f32[12,4,512]{2,1,0:T(4,128)S(1)}, f32[1]{0:T(128)}) custom-call(f32[12,4,512]{2,1,0:T(4,128)S(1)} %copy-done, f32[3,12,4,512]{3,2,1,0:T(4,128)S(1)} %copy-done.1, f32[8,4,512]{2,1,0:T(4,128)S(1)} %copy-done.2, s32[2]{0:T(128)S(1)} %copy-done.5, s32[1,12]{1,0:T(1,128)S(1)} %bitcast.1, f32[3,12]{1,0:T(4,128)S(1)} %copy-done.3, ...), custom_call_target="tpu_custom_call" | custom-call | tf_op jit(solution)/shard_map/pallas_call | solution.py:470
  64.1 0.0 copy-done.7
  64.1 0.7 %fusion = (f32[12,4,512]{2,1,0:T(4,128)}, f32[12,4,512]{2,1,0:T(4,128)}) fusion(f32[12,4,512]{2,1,0:T(4,128)S(1)} %copy-done, f32[12,4,512]{2,1,0:T(4,128)S(1)} %copy-done.7, f32[12,4,512]{2,1,0:T(4,128)S(1)} %get-tuple-element.5), kind=kLoop, calls=%fused_computation.1 | loop fusion | flops 73728 | bytes 491520 | tf_op jit(solution)/shard_map/add | solution.py:513
Async XLA Ops:
  0.6 0.7 copy-start.6
  0.6 0.7 copy-start.5
  1.3 0.9 %copy-start = (f32[12,4,512]{2,1,0:T(4,128)S(1)}, f32[12,4,512]{2,1,0:T(4,128)}, u32[]{:S(2)}) copy-start(f32[12,4,512]{2,1,0:T(4,128)} %lv_ref.1) | copy-start | bytes 294916
  2.2 1.0 %copy-start.1 = (f32[3,12,4,512]{3,2,1,0:T(4,128)S(1)}, f32[3,12,4,512]{3,2,1,0:T(4,128)}, u32[]{:S(2)}) copy-start(f32[3,12,4,512]{3,2,1,0:T(4,128)} %u_ref.1) | copy-start | bytes 884740
  3.2 0.8 %copy-start.2 = (f32[8,4,512]{2,1,0:T(4,128)S(1)}, f32[8,4,512]{2,1,0:T(4,128)}, u32[]{:S(2)}) copy-start(f32[8,4,512]{2,1,0:T(4,128)} %ice_ref.1) | copy-start | bytes 196612
  4.0 0.7 %copy-start.3 = (f32[3,12]{1,0:T(4,128)S(1)}, f32[3,12]{1,0:T(4,128)}, u32[]{:S(2)}) copy-start(f32[3,12]{1,0:T(4,128)} %observed_ref.1) | copy-start | bytes 436
  4.7 0.7 %copy-start.4 = (f32[3,12]{1,0:T(4,128)S(1)}, f32[3,12]{1,0:T(4,128)}, u32[]{:S(2)}) copy-start(f32[3,12]{1,0:T(4,128)} %weight_ref.1) | copy-start | bytes 436
  5.4 58.7 %copy-start.7 = (f32[12,4,512]{2,1,0:T(4,128)S(1)}, f32[12,4,512]{2,1,0:T(4,128)}, u32[]{:S(2)}) copy-start(f32[12,4,512]{2,1,0:T(4,128)} %param.9) | copy-start | bytes 294916

commit v2 on v1

--- a/solution.py
+++ b/solution.py
@@ -54,7 +54,7 @@
         step(i)
         return carry
 
-    lax.fori_loop(first, last, one, 0)
+    lax.fori_loop(first, last, one, 0, unroll=True)
 
 
 def send(src, dst, ssem, rsem, target):
@@ -117,27 +117,42 @@
 
 
 def kernel(
-    lv_ref, u_ref, ice_ref, steps_ref, cells_ref, observed_ref, weight_ref,
+    lv_hbm, u_hbm, ice_hbm, steps_ref, cells_hbm, observed_hbm, weight_hbm,
     grad_ref, misfit_ref,
-    X, E, S1, QA, QO, QR, radS, radR, lvS, lvR,
+    lv_ref, u_ref, ice_ref, cells_ref, observed_ref, weight_ref,
+    X, E, S1, QA, QO, QR, radS, radR, lonS, lonR,
     packet, gathered, block, sites, SB, RB, KH, KL,
-    PB, C1R, C2S, C2R, C3S, C3R, SD, DR, ssem, rsem,
+    PB, C1R, C2S, C2R, C3S, C3R, SD, DR, ssem, rsem, isem,
 ):
     lon, rad = lax.axis_index("lon"), lax.axis_index("rad")
     y, z, c, x = place()
     own_block = y * 2 + c
     right, left = ((lon + 1) % 64, rad), ((lon + 63) % 64, rad)
-    above, below = (lon, (rad + 1) % 8), (lon, (rad + 7) % 8)
+    above, below = (lon, lax.min(rad + 1, 7)), (lon, lax.max(rad - 1, 0))
 
     barrier = pltpu.get_barrier_semaphore()
 
     def greet(target):
         pl.semaphore_signal(barrier, 1, device_id=target, device_id_type=MESH)
 
-    for target in (right, left, above, below):
-        greet(target)
+    has_above, has_below = rad < 7, rad > 0
+    pl.when(has_above)(lambda: greet(above))
+    pl.when(has_below)(lambda: greet(below))
+    greet(right)
+    greet(left)
     repeat(1, 16, lambda i: greet(z_peer(i)[0]))
     repeat(1, 32, lambda i: greet(plane_peer(i)[0]))
+    loads = [
+        pltpu.make_async_copy(source, target, isem.at[k])
+        for k, (source, target) in enumerate((
+            (cells_hbm, cells_ref), (observed_hbm, observed_ref), (weight_hbm, weight_ref),
+            (lv_hbm, lv_ref), (u_hbm, u_ref), (ice_hbm, ice_ref),
+        ))
+    ]
+    for load in loads:
+        load.start()
+    for load in loads:
+        load.wait()
 
     for f in range(4):
         for l in range(COLS):
@@ -146,18 +161,31 @@
             X[f, l + 2, ROWS:16, :] = jnp.zeros((16 - ROWS, NLAT), jnp.float32)
             radS[0, f * 4 + l : f * 4 + l + 1, :] = source[11:12, :]
             radS[1, f * 4 + l : f * 4 + l + 1, :] = source[0:1, :]
+            if l == COLS - 1:
+                lonS[0, f * ROWS : f * ROWS + ROWS, :] = source
+            if l == 0:
+                lonS[1, f * ROWS : f * ROWS + ROWS, :] = source
     packet[...] = jnp.zeros((8, 128), jnp.float32)
     packet[0:1, 0:12] = cells_ref[...].astype(jnp.float32)
     packet[1:4, 0:12] = observed_ref[...]
     packet[4:7, 0:12] = weight_ref[...]
     gathered[z % 8] = packet[...]
-
-    pl.semaphore_wait(barrier, 50)
-
-    send(radS.at[0], radR.at[0], ssem.at[0], rsem.at[0], above)
-    send(radS.at[1], radR.at[1], ssem.at[1], rsem.at[1], below)
-    send(X.at[:, 5], X.at[:, 1], ssem.at[2], rsem.at[2], right)
-    send(X.at[:, 2], X.at[:, 6], ssem.at[3], rsem.at[3], left)
+    nothing = jnp.zeros((16, NLAT), jnp.float32)
+
+    @pl.when(rad == 7)
+    def no_layer_above():
+        radR[1] = nothing
+        radR[3] = nothing
+
+    @pl.when(rad == 0)
+    def no_layer_below():
+        radR[0] = nothing
+        radR[2] = nothing
+
+    pl.semaphore_wait(barrier, 48 + lax.min(rad, 1) + lax.min(7 - rad, 1))
+
+    pl.when(has_above)(lambda: send(radS.at[0], radR.at[0], ssem.at[0], rsem.at[0], above))
+    pl.when(has_below)(lambda: send(radS.at[1], radR.at[1], ssem.at[1], rsem.at[1], below))
 
     def send_record(i):
         target, unused = z_peer((i + 12) % 16)
@@ -165,6 +193,8 @@
 
     repeat(0, 4, send_record)
     repeat(5, 8, send_record)
+    send(lonS.at[0, pl.ds(0, 48)], lonR.at[0, pl.ds(0, 48)], ssem.at[2], rsem.at[2], right)
+    send(lonS.at[1, pl.ds(0, 48)], lonR.at[1, pl.ds(0, 48)], ssem.at[3], rsem.at[3], left)
 
     row = iota((16, NLAT), 0)
     layer = jnp.where(row >= 14, row - 16, row)
@@ -191,12 +221,14 @@
 
     repeat(1, 8, send_block)
 
-    await_bytes(radR.at[0], rsem.at[0])
-    await_bytes(radR.at[1], rsem.at[1])
-    await_bytes(X.at[:, 1], rsem.at[2])
-    await_bytes(X.at[:, 6], rsem.at[3])
-    await_bytes(X.at[:, 5], ssem.at[2])
-    await_bytes(X.at[:, 2], ssem.at[3])
+    await_bytes(lonR.at[0, pl.ds(0, 48)], rsem.at[2])
+    await_bytes(lonR.at[1, pl.ds(0, 48)], rsem.at[3])
+    for f in range(4):
+        for side, p in ((0, 1), (1, 6)):
+            X[f, p, 0:ROWS, :] = lonR[side, f * ROWS : f * ROWS + ROWS, :]
+            X[f, p, ROWS:16, :] = jnp.zeros((16 - ROWS, NLAT), jnp.float32)
+    pl.when(has_below)(lambda: await_bytes(radR.at[0], rsem.at[0]))
+    pl.when(has_above)(lambda: await_bytes(radR.at[1], rsem.at[1]))
     for f in range(4):
         for l in range(COLS):
             X[f, l + 2, 15:16, :] = radR[0, f * 4 + l : f * 4 + l + 1, :]
@@ -275,14 +307,16 @@
     for l in range(COLS):
         radS[2, 12 + l : 13 + l, :] = X[0, l + 2, 10:11, :]
         radS[3, 12 + l : 13 + l, :] = X[0, l + 2, 1:2, :]
-    lvS[0] = jnp.where(own_row, X[0, 4], X[0, 5])
-    lvS[1] = jnp.where(own_row, X[0, 3], X[0, 2])
-    send(radS.at[2], radR.at[2], ssem.at[7], rsem.at[7], above)
-    send(radS.at[3], radR.at[3], ssem.at[8], rsem.at[8], below)
-    send(S1.at[:, 5], S1.at[:, 1], ssem.at[9], rsem.at[9], right)
-    send(S1.at[:, 2], S1.at[:, 6], ssem.at[10], rsem.at[10], left)
-    send(lvS.at[0], lvR.at[0], ssem.at[11], rsem.at[11], right)
-    send(lvS.at[1], lvR.at[1], ssem.at[12], rsem.at[12], left)
+    for side, edge, inner in ((2, 5, 4), (3, 2, 3)):
+        for f in range(3):
+            lonS[side, f * ROWS : f * ROWS + ROWS, :] = S1[f, edge, 0:ROWS, :]
+        lonS[side, 36:48, :] = X[0, inner, 0:ROWS, :]
+        lonS[side, 48:52, :] = X[0, edge, ROWS:16, :]
+        lonS[side, 52:56, :] = jnp.zeros((4, NLAT), jnp.float32)
+    pl.when(has_above)(lambda: send(radS.at[2], radR.at[2], ssem.at[7], rsem.at[7], above))
+    pl.when(has_below)(lambda: send(radS.at[3], radR.at[3], ssem.at[8], rsem.at[8], below))
+    send(lonS.at[2], lonR.at[2], ssem.at[9], rsem.at[9], right)
+    send(lonS.at[3], lonR.at[3], ssem.at[10], rsem.at[10], left)
 
     await_bytes(sites.at[pl.ds(0, 7)], rsem.at[5])
     tiles = blocks_to_lanes([sites[b] for b in range(8)])
@@ -324,7 +358,7 @@
         pred = jnp.where(row8 == f, jnp.broadcast_to(summed, pred.shape), pred)
     pieces = lanes_to_blocks([pred[:, t * 128 : t * 128 + 128] for t in range(6)])
     for b in range(8):
-        PB[b] = pieces[b]
+        PB[b] = pieces[b][0:3]
     C1R[x * 8 + own_block] = PB[own_block]
 
     def send_piece(i):
@@ -343,14 +377,10 @@
 
     repeat(1, 16, send_sum)
 
-    await_bytes(radR.at[2], rsem.at[7])
-    await_bytes(radR.at[3], rsem.at[8])
-    await_bytes(S1.at[:, 1], rsem.at[9])
-    await_bytes(S1.at[:, 6], rsem.at[10])
-    await_bytes(lvR.at[0], rsem.at[11])
-    await_bytes(lvR.at[1], rsem.at[12])
-    await_bytes(S1.at[:, 5], ssem.at[9])
-    await_bytes(S1.at[:, 2], ssem.at[10])
+    pl.when(has_below)(lambda: await_bytes(radR.at[2], rsem.at[7]))
+    pl.when(has_above)(lambda: await_bytes(radR.at[3], rsem.at[8]))
+    await_bytes(lonR.at[2], rsem.at[9])
+    await_bytes(lonR.at[3], rsem.at[10])
     for f in range(3):
         for l in range(COLS):
             S1[f, l + 2, 15:16, :] = radR[2, f * 4 + l : f * 4 + l + 1, :]
@@ -358,9 +388,13 @@
     for l in range(COLS):
         X[0, l + 2, 14:15, :] = radR[2, 12 + l : 13 + l, :]
         X[0, l + 2, 13:14, :] = radR[3, 12 + l : 13 + l, :]
-    for side, far, near in ((0, 0, 1), (1, 7, 6)):
-        X[0, far] = lvR[side]
-        X[0, near] = jnp.where(own_row, X[0, near], lvR[side])
+    for side, far, near in ((2, 0, 1), (3, 7, 6)):
+        for f in range(3):
+            S1[f, near, 0:ROWS, :] = lonR[side, f * ROWS : f * ROWS + ROWS, :]
+            S1[f, near, ROWS:16, :] = jnp.zeros((16 - ROWS, NLAT), jnp.float32)
+        X[0, far, 0:ROWS, :] = lonR[side, 36:48, :]
+        X[0, far, ROWS:16, :] = jnp.zeros((16 - ROWS, NLAT), jnp.float32)
+        X[0, near, ROWS:16, :] = lonR[side, 48:52, :]
     for p in range(8):
         E[p] = jnp.exp(X[0, p])
     for p in range(1, 7):
@@ -370,7 +404,7 @@
         QO[p] = 0.1 / (E[p] + E[p + 1])
 
     await_bytes(C2R.at[pl.ds(0, 15)], rsem.at[14])
-    predicted = jnp.sum(C2R[...], axis=0)
+    predicted = jnp.concatenate([jnp.sum(C2R[...], axis=0), jnp.zeros((5, 128), jnp.float32)], axis=0)
     record = block[...]
     row_of, lane_of = iota((8, 128), 0), iota((8, 128), 1)
     entry = (row_of < 3) & (lane_of < 96)
@@ -378,8 +412,8 @@
     weighted = weight * (predicted - pltpu.roll(record, 7, 0))
     squares = jnp.broadcast_to(jnp.sum(weighted * weighted, axis=0, keepdims=True), (8, 128))
     pulled = jnp.where(row_of == 3, squares, weight * weighted)
-    C3S[...] = pulled
-    C3R[own_block] = pulled
+    C3S[...] = pulled[0:4]
+    C3R[own_block] = pulled[0:4]
 
     def send_pulled(i):
         target, unused = block_peer(i)
@@ -387,7 +421,7 @@
 
     repeat(1, 8, send_pulled)
     await_bytes(C3R.at[pl.ds(0, 7)], rsem.at[15])
-    pulls = [C3R[b] for b in range(8)]
+    pulls = [jnp.concatenate([C3R[b], jnp.zeros((4, 128), jnp.float32)], axis=0) for b in range(8)]
     total = pulls[0]
     for b in range(1, 8):
         total = total + pulls[b]
@@ -401,8 +435,8 @@
 
     first = against(both, KH[...])
     adjoint = (first[0:8] + first[8:16] + against(both, KL[...])[0:8]) * SCALE
-    SD[...] = adjoint
-    DR[x] = adjoint
+    SD[...] = adjoint[0:3]
+    DR[x] = adjoint[0:3]
 
     def send_adjoint(i):
         target, unused = x_peer(i)
@@ -456,9 +490,13 @@
         result = 10.0 * E[p] * whole + 0.1 * X[0, p]
         grad_ref[:, p - 2, :] = result[0:ROWS, :]
 
-    for k, ref in ((0, radS.at[0]), (1, radS.at[1]), (4, gathered.at[pl.ds(0, 7)]), (5, sites.at[pl.ds(0, 7)]), (6, RB.at[pl.ds(0, 3)]),
-                   (7, radS.at[2]), (8, radS.at[3]), (11, lvS.at[0]),
-                   (12, lvS.at[1]), (13, C1R.at[pl.ds(0, 31)]), (14, C2R.at[pl.ds(0, 15)]),
+    pl.when(has_above)(lambda: await_bytes(radS.at[0], ssem.at[0]))
+    pl.when(has_below)(lambda: await_bytes(radS.at[1], ssem.at[1]))
+    pl.when(has_above)(lambda: await_bytes(radS.at[2], ssem.at[7]))
+    pl.when(has_below)(lambda: await_bytes(radS.at[3], ssem.at[8]))
+    for k, ref in ((2, lonS.at[0, pl.ds(0, 48)]), (3, lonS.at[1, pl.ds(0, 48)]), (4, gathered.at[pl.ds(0, 7)]),
+                   (5, sites.at[pl.ds(0, 7)]), (6, RB.at[pl.ds(0, 3)]), (9, lonS.at[2]), (10, lonS.at[3]),
+                   (13, C1R.at[pl.ds(0, 31)]), (14, C2R.at[pl.ds(0, 15)]),
                    (15, C3R.at[pl.ds(0, 7)]), (16, DR.at[pl.ds(0, 3)])):
         await_bytes(ref, ssem.at[k])
 
@@ -467,15 +505,22 @@
     f32 = jnp.float32
     vmem = pl.BlockSpec(memory_space=pltpu.VMEM)
     smem = pl.BlockSpec(memory_space=pltpu.SMEM)
+    hbm = pl.BlockSpec(memory_space=pltpu.HBM)
     gradient, misfit = pl.pallas_call(
         kernel,
         out_shape=(
             jax.ShapeDtypeStruct((ROWS, COLS, NLAT), f32),
             jax.ShapeDtypeStruct((1,), f32),
         ),
-        in_specs=[vmem, vmem, vmem, smem, vmem, vmem, vmem],
+        in_specs=[hbm, hbm, hbm, smem, hbm, hbm, hbm],
         out_specs=(vmem, smem),
         scratch_shapes=[
+            pltpu.VMEM((ROWS, COLS, NLAT), f32),
+            pltpu.VMEM((3, ROWS, COLS, NLAT), f32),
+            pltpu.VMEM((8, COLS, NLAT), f32),
+            pltpu.VMEM((1, 12), jnp.int32),
+            pltpu.VMEM((3, 12), f32),
+            pltpu.VMEM((3, 12), f32),
             pltpu.VMEM((4, 8, 16, NLAT), f32),
             pltpu.VMEM((8, 16, NLAT), f32),
             pltpu.VMEM((3, 8, 16, NLAT), f32),
@@ -484,8 +529,8 @@
             pltpu.VMEM((8, 16, NLAT), f32),
             pltpu.VMEM((4, 16, NLAT), f32),
             pltpu.VMEM((4, 16, NLAT), f32),
-            pltpu.VMEM((2, 16, NLAT), f32),
-            pltpu.VMEM((2, 16, NLAT), f32),
+            pltpu.VMEM((4, 56, NLAT), f32),
+            pltpu.VMEM((4, 56, NLAT), f32),
             pltpu.VMEM((8, 128), f32),
             pltpu.VMEM((8, 8, 128), f32),
             pltpu.VMEM((8, 128), f32),
@@ -494,19 +539,20 @@
             pltpu.VMEM((4, 24, 128), f32),
             pltpu.VMEM((1024, 768), jnp.bfloat16),
             pltpu.VMEM((1024, 768), jnp.bfloat16),
-            pltpu.VMEM((8, 8, 128), f32),
-            pltpu.VMEM((32, 8, 128), f32),
-            pltpu.VMEM((8, 128), f32),
-            pltpu.VMEM((16, 8, 128), f32),
-            pltpu.VMEM((8, 128), f32),
-            pltpu.VMEM((8, 8, 128), f32),
-            pltpu.VMEM((8, 1024), f32),
-            pltpu.VMEM((4, 8, 1024), f32),
+            pltpu.VMEM((8, 3, 128), f32),
+            pltpu.VMEM((32, 3, 128), f32),
+            pltpu.VMEM((3, 128), f32),
+            pltpu.VMEM((16, 3, 128), f32),
+            pltpu.VMEM((4, 128), f32),
+            pltpu.VMEM((8, 4, 128), f32),
+            pltpu.VMEM((3, 1024), f32),
+            pltpu.VMEM((4, 3, 1024), f32),
             pltpu.SemaphoreType.DMA((17,)),
             pltpu.SemaphoreType.DMA((17,)),
+            pltpu.SemaphoreType.DMA((6,)),
         ],
         compiler_params=pltpu.CompilerParams(
-            collective_id=0, has_side_effects=True, vmem_limit_bytes=48 * 1024 * 1024
+            collective_id=0, has_side_effects=True, vmem_limit_bytes=62 * 1024 * 1024
         ),
     )(logvisc, displacement, ice_history, load_steps, site_cells.reshape(1, 12), observed, site_weight)
     half_momentum = momentum - 0.5 * gradient

time: 66.9 us -> 60.1 us (0.90)
  local copies, waits for them, and re-layouts: 4.71 us -> 0.01 us
  Pallas kernels: 58.7 us -> 55.9 us
  other arithmetic: 0.73 us -> 1.62 us
    unnamed x16 -> x4, local copies, waits for them, and re-layouts: 4.71 us -> 0.01 us
    pallas_call x1, Pallas kernels: 58.7 us -> 55.9 us  [body(): pl.pallas_call(kernel, out_shape=(jax.ShapeDtypeStruct((ROWS, COLS, NLAT)...]
    add x1, other arithmetic: 0.73 us -> 1.62 us  [body(): return (logvisc + half_momentum, half_momentum, misfit)]
where the time goes in v2:
time: 60.1 us; the launch traced here: 59.9 us
  Pallas kernels  55.9 us (93%)
  between operations  2.43 us (4%)
  other arithmetic  1.62 us (3%)
    pallas_call x1, Pallas kernels, body(): pl.pallas_call(kernel, out_shape=(jax.ShapeDtypeStruct((ROWS, COLS, NLAT)...  55.9 us
    add x1, other arithmetic, body(): return (logvisc + half_momentum, half_momentum, misfit)  1.62 us

profile of v2, /device:TPU:1, one launch (start us, length us, event | category | flops | bytes accessed | tf_op | source)
XLA Modules:
  0.0 59.9 jit_solution(13155613467562525037)
XLA Ops:
  0.6 0.0 copy-start
  0.6 0.0 copy-start.1
  0.7 55.9 %shard_map.103 = (f32[12,4,512]{2,1,0:T(4,128)}, f32[1]{0:T(128)}) custom-call(f32[12,4,512]{2,1,0:T(4,128)} %lv_hbm.1, f32[3,12,4,512]{3,2,1,0:T(4,128)} %u_hbm.1, f32[8,4,512]{2,1,0:T(4,128)} %ice_hbm.1, s32[2]{0:T(128)} %steps_ref.1, s32[1,12]{1,0:T(1,128)} %bitcast.1, f32[3,12]{1,0:T(4,128)} %observed_hbm.1, f32[3,12]{1,0:T(4,128)} %weight_hbm.1), custom_call_target="tpu_custom_call" | custom-call | tf_op jit(solution)/shard_map/pallas_call | solution.py:509
  56.5 0.0 copy-done
  56.5 0.0 copy-done.1
  56.5 1.6 %fusion = (f32[12,4,512]{2,1,0:T(4,128)}, f32[12,4,512]{2,1,0:T(4,128)}) fusion(f32[12,4,512]{2,1,0:T(4,128)S(1)} %copy-done, f32[12,4,512]{2,1,0:T(4,128)S(1)} %copy-done.1, f32[12,4,512]{2,1,0:T(4,128)} %get-tuple-element.5), kind=kLoop, calls=%fused_computation.1 | loop fusion | flops 73728 | bytes 491520 | tf_op jit(solution)/shard_map/add | solution.py:559
Async XLA Ops:
  0.6 55.9 %copy-start = (f32[12,4,512]{2,1,0:T(4,128)S(1)}, f32[12,4,512]{2,1,0:T(4,128)}, u32[]{:S(2)}) copy-start(f32[12,4,512]{2,1,0:T(4,128)} %lv_hbm.1) | copy-start | bytes 294916
  0.6 55.9 %copy-start.1 = (f32[12,4,512]{2,1,0:T(4,128)S(1)}, f32[12,4,512]{2,1,0:T(4,128)}, u32[]{:S(2)}) copy-start(f32[12,4,512]{2,1,0:T(4,128)} %param.9) | copy-start | bytes 294916

commit v3 on v2

--- a/solution.py
+++ b/solution.py
@@ -50,11 +50,16 @@
 
 
 def repeat(first, last, step):
-    def one(i, carry):
+    for i in range(first, last):
         step(i)
-        return carry
-
-    lax.fori_loop(first, last, one, 0, unroll=True)
+
+
+def ring(offset, size):
+    return min(offset % size, size - offset % size)
+
+
+FAR_Z = sorted(range(1, 16), key=lambda i: -ring(i, 16))
+FAR_PLANE = sorted(range(1, 32), key=lambda i: -(ring(i, 4) + ring(i // 4, 4) + 0.5 * (i // 16)))
 
 
 def send(src, dst, ssem, rsem, target):
@@ -122,7 +127,8 @@
     lv_ref, u_ref, ice_ref, cells_ref, observed_ref, weight_ref,
     X, E, S1, QA, QO, QR, radS, radR, lonS, lonR,
     packet, gathered, block, sites, SB, RB, KH, KL,
-    PB, C1R, C2S, C2R, C3S, C3R, SD, DR, ssem, rsem, isem,
+    PB, C1R, C2S, C2R, C3S, C3R, SD, DR,
+    TH, TL, AS, AA, AL, AO, UO, SO, UA, SA, UR, SR, ssem, rsem, isem,
 ):
     lon, rad = lax.axis_index("lon"), lax.axis_index("rad")
     y, z, c, x = place()
@@ -140,8 +146,10 @@
     pl.when(has_below)(lambda: greet(below))
     greet(right)
     greet(left)
-    repeat(1, 16, lambda i: greet(z_peer(i)[0]))
-    repeat(1, 32, lambda i: greet(plane_peer(i)[0]))
+    for i in FAR_Z:
+        greet(z_peer(i)[0])
+    for i in FAR_PLANE:
+        greet(plane_peer(i)[0])
     loads = [
         pltpu.make_async_copy(source, target, isem.at[k])
         for k, (source, target) in enumerate((
@@ -347,10 +355,12 @@
     await_bytes(RB.at[pl.ds(0, 3)], rsem.at[6])
     band = (RB[0] + RB[1]) + (RB[2] + RB[3])
     place_of = iota((24, 128), 0) % 8
-    wide = jnp.concatenate([jnp.where(place_of == p, band, 0.0) for p in range(8)], axis=1)
+    wide = jnp.concatenate([jnp.where(place_of == p, band, 0.0) for p in range(1, 7)], axis=1)
     high, low = split(wide)
     dot = functools.partial(jnp.dot, preferred_element_type=jnp.float32)
-    parts = dot(high, KH[...]) + dot(high, KL[...]) + dot(low, KH[...])
+    both = jnp.concatenate([high.astype(jnp.float32), low.astype(jnp.float32)], axis=0).astype(jnp.bfloat16)
+    parts = dot(both, KH[128:896])
+    parts = parts[0:24] + parts[24:48] + dot(high, KL[128:896])
     row8 = iota((8, 6 * 128), 0)
     pred = jnp.zeros((8, 6 * 128), jnp.float32)
     for f in range(3):
@@ -365,7 +375,8 @@
         target, unused, b2 = plane_peer(i)
         send(PB.at[b2], C1R.at[x * 8 + own_block], ssem.at[13], rsem.at[13], target)
 
-    repeat(1, 32, send_piece)
+    for i in FAR_PLANE:
+        send_piece(i)
     await_bytes(C1R.at[pl.ds(0, 31)], rsem.at[13])
     summed = jnp.sum(C1R[...], axis=0)
     C2S[...] = summed
@@ -375,7 +386,8 @@
         target, unused = z_peer(i)
         send(C2S, C2R.at[z], ssem.at[14], rsem.at[14], target)
 
-    repeat(1, 16, send_sum)
+    for i in FAR_Z:
+        send_sum(i)
 
     pl.when(has_below)(lambda: await_bytes(radR.at[2], rsem.at[7]))
     pl.when(has_above)(lambda: await_bytes(radR.at[3], rsem.at[8]))
@@ -402,6 +414,30 @@
         QR[p] = edge_rad(E[p])
     for p in range(7):
         QO[p] = 0.1 / (E[p] + E[p + 1])
+    for p in range(1, 7):
+        slope = QR[p] * (wr_next - wr)
+        AS[p] = wr + slope - last_row(slope)
+        along = QA[p] * wr
+        AA[p] = along
+        AL[p] = last_lat(along)
+    for p in range(7):
+        AO[p] = QO[p] * wr
+    for f in range(3):
+        for p in range(1, 6):
+            u, s, square = X[f + 1, p], S1[f, p], QO[p] * QO[p]
+            UO[f, p] = square * (X[f + 1, p + 1] - u)
+            SO[f, p] = square * wr * (S1[f, p + 1] - s)
+            if p > 1:
+                square = QA[p] * QA[p]
+                UA[f, p] = square * (next_lat(u) - u)
+                SA[f, p] = square * wr * (next_lat(s) - s)
+                square = QR[p] * QR[p]
+                UR[f, p] = square * (next_row(u) - u)
+                SR[f, p] = square * (wr_next - wr) * (next_row(s) - s)
+    for t in range(6):
+        for p in range(8):
+            TH[t * 128 : t * 128 + 128, p * 128 : p * 128 + 128] = KH[p * 128 : p * 128 + 128, t * 128 : t * 128 + 128].T
+            TL[t * 128 : t * 128 + 128, p * 128 : p * 128 + 128] = KL[p * 128 : p * 128 + 128, t * 128 : t * 128 + 128].T
 
     await_bytes(C2R.at[pl.ds(0, 15)], rsem.at[14])
     predicted = jnp.concatenate([jnp.sum(C2R[...], axis=0), jnp.zeros((5, 128), jnp.float32)], axis=0)
@@ -430,13 +466,12 @@
     high, low = split(pull)
     both = jnp.concatenate([high, low], axis=0)
 
-    def against(lhs, rhs):
-        return lax.dot_general(lhs, rhs, (((1,), (1,)), ((), ())), preferred_element_type=jnp.float32)
-
-    first = against(both, KH[...])
-    adjoint = (first[0:8] + first[8:16] + against(both, KL[...])[0:8]) * SCALE
-    SD[...] = adjoint[0:3]
-    DR[x] = adjoint[0:3]
+    first = dot(both, TH[...])
+    adjoint = (first[0:8] + first[8:16] + dot(both, TL[...])[0:8]) * SCALE
+    for f in range(3):
+        for p in range(8):
+            SD[f * 8 + p : f * 8 + p + 1, :] = adjoint[f : f + 1, p * 128 : p * 128 + 128]
+    DR[x] = SD[...]
 
     def send_adjoint(i):
         target, unused = x_peer(i)
@@ -448,44 +483,28 @@
     faces_a = [jnp.zeros((16, NLAT), jnp.float32) for unused in range(8)]
     faces_r = [jnp.zeros((16, NLAT), jnp.float32) for unused in range(8)]
     faces_o = [jnp.zeros((16, NLAT), jnp.float32) for unused in range(8)]
-    for f in range(3):
-        a2 = []
-        for p in range(8):
-            surface = jnp.concatenate(
-                [DR[band, f : f + 1, p * 128 : p * 128 + 128] for band in range(4)], axis=1
-            )
-            a2.append(wr * jnp.broadcast_to(surface, (16, NLAT)))
+
+    def spread(v, p):
+        return jnp.broadcast_to(v[p : p + 1, :], (16, NLAT))
+
+    for f in range(3):
+        surface = jnp.concatenate([DR[band, f * 8 : f * 8 + 8, :] for band in range(4)], axis=1)
+        step = next_lat(surface) - surface
+        step_before = last_lat(step)
+        beside = [spread(surface, p + 1) - spread(surface, p) for p in range(7)]
         a1 = [None] * 8
         for p in range(1, 7):
-            flux = QA[p] * (next_lat(a2[p]) - a2[p])
-            rise = QR[p] * (next_row(a2[p]) - a2[p])
             a1[p] = (
-                a2[p] + (flux - last_lat(flux)) + (rise - last_row(rise))
-                + QO[p] * (a2[p + 1] - a2[p]) + QO[p - 1] * (a2[p - 1] - a2[p])
+                AS[p] * spread(surface, p) + AA[p] * spread(step, p) - AL[p] * spread(step_before, p)
+                + AO[p] * beside[p] - AO[p - 1] * beside[p - 1]
             )
         for p in range(1, 6):
-            u, s = X[f + 1, p], S1[f, p]
-            faces_o[p] = (
-                faces_o[p]
-                + (X[f + 1, p + 1] - u) * (a1[p + 1] - a1[p])
-                + (S1[f, p + 1] - s) * (a2[p + 1] - a2[p])
-            )
+            faces_o[p] = faces_o[p] + UO[f, p] * (a1[p + 1] - a1[p]) + SO[f, p] * beside[p]
             if p > 1:
-                faces_a[p] = (
-                    faces_a[p]
-                    + (next_lat(u) - u) * (next_lat(a1[p]) - a1[p])
-                    + (next_lat(s) - s) * (next_lat(a2[p]) - a2[p])
-                )
-                faces_r[p] = (
-                    faces_r[p]
-                    + (next_row(u) - u) * (next_row(a1[p]) - a1[p])
-                    + (next_row(s) - s) * (next_row(a2[p]) - a2[p])
-                )
-    for p in range(1, 6):
-        faces_o[p] = QO[p] * QO[p] * faces_o[p]
+                faces_a[p] = faces_a[p] + UA[f, p] * (next_lat(a1[p]) - a1[p]) + SA[f, p] * spread(step, p)
+                faces_r[p] = faces_r[p] + UR[f, p] * (next_row(a1[p]) - a1[p]) + SR[f, p] * spread(surface, p)
     for p in range(2, 6):
-        along = QA[p] * QA[p] * faces_a[p]
-        upward = QR[p] * QR[p] * faces_r[p]
+        along, upward = faces_a[p], faces_r[p]
         whole = (along + last_lat(along)) + (upward + last_row(upward)) + (faces_o[p] + faces_o[p - 1])
         result = 10.0 * E[p] * whole + 0.1 * X[0, p]
         grad_ref[:, p - 2, :] = result[0:ROWS, :]
@@ -509,7 +528,7 @@
     gradient, misfit = pl.pallas_call(
         kernel,
         out_shape=(
-            jax.ShapeDtypeStruct((ROWS, COLS, NLAT), f32),
+            pltpu.VMEM((ROWS, COLS, NLAT), f32),
             jax.ShapeDtypeStruct((1,), f32),
         ),
         in_specs=[hbm, hbm, hbm, smem, hbm, hbm, hbm],
@@ -545,8 +564,20 @@
             pltpu.VMEM((16, 3, 128), f32),
             pltpu.VMEM((4, 128), f32),
             pltpu.VMEM((8, 4, 128), f32),
-            pltpu.VMEM((3, 1024), f32),
-            pltpu.VMEM((4, 3, 1024), f32),
+            pltpu.VMEM((24, 128), f32),
+            pltpu.VMEM((4, 24, 128), f32),
+            pltpu.VMEM((768, 1024), jnp.bfloat16),
+            pltpu.VMEM((768, 1024), jnp.bfloat16),
+            pltpu.VMEM((8, 16, NLAT), f32),
+            pltpu.VMEM((8, 16, NLAT), f32),
+            pltpu.VMEM((8, 16, NLAT), f32),
+            pltpu.VMEM((8, 16, NLAT), f32),
+            pltpu.VMEM((3, 8, 16, NLAT), f32),
+            pltpu.VMEM((3, 8, 16, NLAT), f32),
+            pltpu.VMEM((3, 8, 16, NLAT), f32),
+            pltpu.VMEM((3, 8, 16, NLAT), f32),
+            pltpu.VMEM((3, 8, 16, NLAT), f32),
+            pltpu.VMEM((3, 8, 16, NLAT), f32),
             pltpu.SemaphoreType.DMA((17,)),
             pltpu.SemaphoreType.DMA((17,)),
             pltpu.SemaphoreType.DMA((6,)),

time: 60.1 us -> 56.8 us (0.945)
  Pallas kernels: 55.9 us -> 53.5 us
  other arithmetic: 1.62 us -> 0.73 us
    pallas_call x1, Pallas kernels: 55.9 us -> 53.5 us  [body(): pl.pallas_call(kernel, out_shape=(pltpu.VMEM((ROWS, COLS, NLAT), f32), ja...]
    add x1, other arithmetic: 1.62 us -> 0.73 us  [body(): return (logvisc + half_momentum, half_momentum, misfit)]
where the time goes in v3:
time: 56.8 us; the launch traced here: 56.6 us
  Pallas kernels  53.5 us (94%)
  between operations  2.41 us (4%)
  other arithmetic  0.73 us (1%)
    pallas_call x1, Pallas kernels, body(): pl.pallas_call(kernel, out_shape=(pltpu.VMEM((ROWS, COLS, NLAT), f32), ja...  53.5 us

profile of v3, /device:TPU:1, one launch (start us, length us, event | category | flops | bytes accessed | tf_op | source)
XLA Modules:
  0.0 56.6 jit_solution(17664947496968756400)
XLA Ops:
  0.6 0.0 copy-start
  0.6 0.0 copy-start.1
  0.7 53.5 %shard_map.103 = (f32[12,4,512]{2,1,0:T(4,128)S(1)}, f32[1]{0:T(128)}) custom-call(f32[12,4,512]{2,1,0:T(4,128)} %lv_hbm.1, f32[3,12,4,512]{3,2,1,0:T(4,128)} %u_hbm.1, f32[8,4,512]{2,1,0:T(4,128)} %ice_hbm.1, s32[2]{0:T(128)} %steps_ref.1, s32[1,12]{1,0:T(1,128)} %bitcast.1, f32[3,12]{1,0:T(4,128)} %observed_hbm.1, f32[3,12]{1,0:T(4,128)} %weight_hbm.1), custom_call_target="tpu_custom_call" | custom-call | tf_op jit(solution)/shard_map/pallas_call | solution.py:528
  54.1 0.0 copy-done
  54.1 0.0 copy-done.1
  54.1 0.7 %fusion = (f32[12,4,512]{2,1,0:T(4,128)}, f32[12,4,512]{2,1,0:T(4,128)}) fusion(f32[12,4,512]{2,1,0:T(4,128)S(1)} %copy-done, f32[12,4,512]{2,1,0:T(4,128)S(1)} %copy-done.1, f32[12,4,512]{2,1,0:T(4,128)S(1)} %get-tuple-element.5), kind=kLoop, calls=%fused_computation.1 | loop fusion | flops 73728 | bytes 491520 | tf_op jit(solution)/shard_map/add | solution.py:590
Async XLA Ops:
  0.6 53.5 %copy-start = (f32[12,4,512]{2,1,0:T(4,128)S(1)}, f32[12,4,512]{2,1,0:T(4,128)}, u32[]{:S(2)}) copy-start(f32[12,4,512]{2,1,0:T(4,128)} %lv_hbm.1) | copy-start | bytes 294916
  0.6 53.5 %copy-start.1 = (f32[12,4,512]{2,1,0:T(4,128)S(1)}, f32[12,4,512]{2,1,0:T(4,128)}, u32[]{:S(2)}) copy-start(f32[12,4,512]{2,1,0:T(4,128)} %param.9) | copy-start | bytes 294916

commit v4 on v3

--- a/solution.py
+++ b/solution.py
@@ -59,6 +59,7 @@
 
 
 FAR_Z = sorted(range(1, 16), key=lambda i: -ring(i, 16))
+NEAR_Z = [i for i in FAR_Z if ring(i, 16) <= 4]
 FAR_PLANE = sorted(range(1, 32), key=lambda i: -(ring(i, 4) + ring(i // 4, 4) + 0.5 * (i // 16)))
 
 
@@ -102,18 +103,6 @@
         high = pltpu.roll(blocks[b + 1], second % 128, 1)
         tiles.append(jnp.where(lane < second, low, high))
     return tiles
-
-
-def lanes_to_blocks(tiles):
-    lane = iota((8, 128), 1)
-    blocks = []
-    for b in range(8):
-        t, offset = (96 * b) // 128, (96 * b) % 128
-        block = pltpu.roll(tiles[t], 128 - offset, 1) if offset else tiles[t]
-        if offset > 32:
-            block = jnp.where(lane < 128 - offset, block, pltpu.roll(tiles[t + 1], 128 - offset, 1))
-        blocks.append(jnp.where(lane < 96, block, 0.0))
-    return blocks
 
 
 def split(v):
@@ -146,7 +135,7 @@
     pl.when(has_below)(lambda: greet(below))
     greet(right)
     greet(left)
-    for i in FAR_Z:
+    for i in NEAR_Z:
         greet(z_peer(i)[0])
     for i in FAR_PLANE:
         greet(plane_peer(i)[0])
@@ -190,7 +179,7 @@
         radR[0] = nothing
         radR[2] = nothing
 
-    pl.semaphore_wait(barrier, 48 + lax.min(rad, 1) + lax.min(7 - rad, 1))
+    pl.semaphore_wait(barrier, 41 + lax.min(rad, 1) + lax.min(7 - rad, 1))
 
     pl.when(has_above)(lambda: send(radS.at[0], radR.at[0], ssem.at[0], rsem.at[0], above))
     pl.when(has_below)(lambda: send(radS.at[1], radR.at[1], ssem.at[1], rsem.at[1], below))
@@ -201,8 +190,9 @@
 
     repeat(0, 4, send_record)
     repeat(5, 8, send_record)
-    send(lonS.at[0, pl.ds(0, 48)], lonR.at[0, pl.ds(0, 48)], ssem.at[2], rsem.at[2], right)
-    send(lonS.at[1, pl.ds(0, 48)], lonR.at[1, pl.ds(0, 48)], ssem.at[3], rsem.at[3], left)
+    for side in (1 - c, c):
+        target = (lax.rem(lon + 65 - 2 * side, 64), rad)
+        send(lonS.at[side, pl.ds(0, 48)], lonR.at[side, pl.ds(0, 48)], ssem.at[2 + side], rsem.at[2 + side], target)
 
     row = iota((16, NLAT), 0)
     layer = jnp.where(row >= 14, row - 16, row)
@@ -366,14 +356,14 @@
     for f in range(3):
         summed = jnp.sum(parts[f * 8 : f * 8 + 8, :], axis=0, keepdims=True) * SCALE
         pred = jnp.where(row8 == f, jnp.broadcast_to(summed, pred.shape), pred)
-    pieces = lanes_to_blocks([pred[:, t * 128 : t * 128 + 128] for t in range(6)])
-    for b in range(8):
-        PB[b] = pieces[b][0:3]
-    C1R[x * 8 + own_block] = PB[own_block]
+    for half in range(2):
+        for f in range(3):
+            PB[half, :, f * 384 : f * 384 + 384] = pred[f : f + 1, half * 384 : half * 384 + 384]
+    C1R[x * 8 + own_block] = PB[c]
 
     def send_piece(i):
         target, unused, b2 = plane_peer(i)
-        send(PB.at[b2], C1R.at[x * 8 + own_block], ssem.at[13], rsem.at[13], target)
+        send(PB.at[b2 % 2], C1R.at[x * 8 + own_block], ssem.at[13], rsem.at[13], target)
 
     for i in FAR_PLANE:
         send_piece(i)
@@ -439,30 +429,25 @@
             TH[t * 128 : t * 128 + 128, p * 128 : p * 128 + 128] = KH[p * 128 : p * 128 + 128, t * 128 : t * 128 + 128].T
             TL[t * 128 : t * 128 + 128, p * 128 : p * 128 + 128] = KL[p * 128 : p * 128 + 128, t * 128 : t * 128 + 128].T
 
+    record = jnp.where(c == 0, jnp.concatenate(tiles[0:3], axis=1), jnp.concatenate(tiles[3:6], axis=1))
+    row_of = iota((8, 384), 0)
+    weight = jnp.where(row_of < 3, pltpu.roll(record, 4, 0), 0.0)
+    aim = pltpu.roll(record, 7, 0)
+
     await_bytes(C2R.at[pl.ds(0, 15)], rsem.at[14])
-    predicted = jnp.concatenate([jnp.sum(C2R[...], axis=0), jnp.zeros((5, 128), jnp.float32)], axis=0)
-    record = block[...]
-    row_of, lane_of = iota((8, 128), 0), iota((8, 128), 1)
-    entry = (row_of < 3) & (lane_of < 96)
-    weight = jnp.where(entry, pltpu.roll(record, 4, 0), 0.0)
-    weighted = weight * (predicted - pltpu.roll(record, 7, 0))
-    squares = jnp.broadcast_to(jnp.sum(weighted * weighted, axis=0, keepdims=True), (8, 128))
+    total = jnp.sum(C2R[...], axis=0)
+    predicted = jnp.concatenate(
+        [total[:, f * 384 : f * 384 + 384] for f in range(3)] + [jnp.zeros((5, 384), jnp.float32)], axis=0
+    )
+    weighted = weight * (predicted - aim)
+    squares = jnp.broadcast_to(jnp.sum(weighted * weighted, axis=0, keepdims=True), (8, 384))
     pulled = jnp.where(row_of == 3, squares, weight * weighted)
     C3S[...] = pulled[0:4]
-    C3R[own_block] = pulled[0:4]
-
-    def send_pulled(i):
-        target, unused = block_peer(i)
-        send(C3S, C3R.at[own_block], ssem.at[15], rsem.at[15], target)
-
-    repeat(1, 8, send_pulled)
-    await_bytes(C3R.at[pl.ds(0, 7)], rsem.at[15])
-    pulls = [jnp.concatenate([C3R[b], jnp.zeros((4, 128), jnp.float32)], axis=0) for b in range(8)]
-    total = pulls[0]
-    for b in range(1, 8):
-        total = total + pulls[b]
-    misfit_ref[0] = jnp.sum(total[3:4, :]) / (3.0 * 768.0)
-    pull = jnp.concatenate(blocks_to_lanes(pulls), axis=1)
+    C3R[c] = pulled[0:4]
+    send(C3S, C3R.at[c], ssem.at[15], rsem.at[15], device(y, z, 1 - c, x))
+    await_bytes(C3R.at[0], rsem.at[15])
+    pull = jnp.concatenate([C3R[0], C3R[1]], axis=1)
+    pull = jnp.concatenate([pull, jnp.zeros((4, 768), jnp.float32)], axis=0)
     high, low = split(pull)
     both = jnp.concatenate([high, low], axis=0)
 
@@ -478,6 +463,7 @@
         send(SD, DR.at[x], ssem.at[16], rsem.at[16], target)
 
     repeat(1, 4, send_adjoint)
+    misfit_ref[0] = jnp.sum(C3R[0, 3:4, :] + C3R[1, 3:4, :]) / (3.0 * 768.0)
     await_bytes(DR.at[pl.ds(0, 3)], rsem.at[16])
 
     faces_a = [jnp.zeros((16, NLAT), jnp.float32) for unused in range(8)]
@@ -516,7 +502,7 @@
     for k, ref in ((2, lonS.at[0, pl.ds(0, 48)]), (3, lonS.at[1, pl.ds(0, 48)]), (4, gathered.at[pl.ds(0, 7)]),
                    (5, sites.at[pl.ds(0, 7)]), (6, RB.at[pl.ds(0, 3)]), (9, lonS.at[2]), (10, lonS.at[3]),
                    (13, C1R.at[pl.ds(0, 31)]), (14, C2R.at[pl.ds(0, 15)]),
-                   (15, C3R.at[pl.ds(0, 7)]), (16, DR.at[pl.ds(0, 3)])):
+                   (15, C3S), (16, DR.at[pl.ds(0, 3)])):
         await_bytes(ref, ssem.at[k])
 
 
@@ -558,12 +544,12 @@
             pltpu.VMEM((4, 24, 128), f32),
             pltpu.VMEM((1024, 768), jnp.bfloat16),
             pltpu.VMEM((1024, 768), jnp.bfloat16),
-            pltpu.VMEM((8, 3, 128), f32),
-            pltpu.VMEM((32, 3, 128), f32),
-            pltpu.VMEM((3, 128), f32),
-            pltpu.VMEM((16, 3, 128), f32),
-            pltpu.VMEM((4, 128), f32),
-            pltpu.VMEM((8, 4, 128), f32),
+            pltpu.VMEM((2, 1, 1152), f32),
+            pltpu.VMEM((32, 1, 1152), f32),
+            pltpu.VMEM((1, 1152), f32),
+            pltpu.VMEM((16, 1, 1152), f32),
+            pltpu.VMEM((4, 384), f32),
+            pltpu.VMEM((2, 4, 384), f32),
             pltpu.VMEM((24, 128), f32),
             pltpu.VMEM((4, 24, 128), f32),
             pltpu.VMEM((768, 1024), jnp.bfloat16),

time: 56.8 us -> 55.2 us (0.972)
  Pallas kernels: 53.5 us -> 51.8 us
    pallas_call x1, Pallas kernels: 53.5 us -> 51.8 us  [body(): pl.pallas_call(kernel, out_shape=(pltpu.VMEM((ROWS, COLS, NLAT), f32), ja...]
where the time goes in v4:
time: 55.2 us; the launch traced here: 55 us
  Pallas kernels  51.8 us (94%)
  between operations  2.41 us (4%)
  other arithmetic  0.73 us (1%)
    pallas_call x1, Pallas kernels, body(): pl.pallas_call(kernel, out_shape=(pltpu.VMEM((ROWS, COLS, NLAT), f32), ja...  51.8 us

profile of v4, /device:TPU:1, one launch (start us, length us, event | category | flops | bytes accessed | tf_op | source)
XLA Modules:
  0.0 55.0 jit_solution(6716321391672171006)
XLA Ops:
  0.6 0.0 copy-start
  0.6 0.0 copy-start.1
  0.7 51.8 %shard_map.103 = (f32[12,4,512]{2,1,0:T(4,128)S(1)}, f32[1]{0:T(128)}) custom-call(f32[12,4,512]{2,1,0:T(4,128)} %lv_hbm.1, f32[3,12,4,512]{3,2,1,0:T(4,128)} %u_hbm.1, f32[8,4,512]{2,1,0:T(4,128)} %ice_hbm.1, s32[2]{0:T(128)} %steps_ref.1, s32[1,12]{1,0:T(1,128)} %bitcast.1, f32[3,12]{1,0:T(4,128)} %observed_hbm.1, f32[3,12]{1,0:T(4,128)} %weight_hbm.1), custom_call_target="tpu_custom_call" | custom-call | tf_op jit(solution)/shard_map/pallas_call | solution.py:514
  52.5 0.0 copy-done
  52.5 0.0 copy-done.1
  52.5 0.7 %fusion = (f32[12,4,512]{2,1,0:T(4,128)}, f32[12,4,512]{2,1,0:T(4,128)}) fusion(f32[12,4,512]{2,1,0:T(4,128)S(1)} %copy-done, f32[12,4,512]{2,1,0:T(4,128)S(1)} %copy-done.1, f32[12,4,512]{2,1,0:T(4,128)S(1)} %get-tuple-element.5), kind=kLoop, calls=%fused_computation.1 | loop fusion | flops 73728 | bytes 491520 | tf_op jit(solution)/shard_map/add | solution.py:576
Async XLA Ops:
  0.6 51.9 %copy-start = (f32[12,4,512]{2,1,0:T(4,128)S(1)}, f32[12,4,512]{2,1,0:T(4,128)}, u32[]{:S(2)}) copy-start(f32[12,4,512]{2,1,0:T(4,128)} %lv_hbm.1) | copy-start | bytes 294916
  0.6 51.9 %copy-start.1 = (f32[12,4,512]{2,1,0:T(4,128)S(1)}, f32[12,4,512]{2,1,0:T(4,128)}, u32[]{:S(2)}) copy-start(f32[12,4,512]{2,1,0:T(4,128)} %param.9) | copy-start | bytes 294916

commit v5 on v4

--- a/solution.py
+++ b/solution.py
@@ -206,6 +206,23 @@
     not_last = iota((16, NLAT), 1) < NLAT - 1
     is_top = jnp.where(rad == 7, 1.0, 0.0)
 
+    def edge_lat(e):
+        return jnp.where(not_last, 0.1 / (e + next_lat(e)), 0.0)
+
+    for p in range(2, 6):
+        E[p] = jnp.exp(X[0, p])
+        QA[p] = edge_lat(E[p])
+        for f in range(3):
+            u = X[f + 1, p]
+            flux = QA[p] * (next_lat(u) - u)
+            S1[f, p] = u + (flux - last_lat(flux))
+    for p in range(2, 5):
+        QO[p] = 0.1 / (E[p] + E[p + 1])
+        for f in range(3):
+            flow = QO[p] * (X[f + 1, p + 1] - X[f + 1, p])
+            S1[f, p] = S1[f, p] + flow
+            S1[f, p + 1] = S1[f, p + 1] - flow
+
     await_bytes(gathered.at[pl.ds(0, 7)], rsem.at[4])
     record = gathered[0]
     for slot in range(1, 8):
@@ -232,27 +249,25 @@
             X[f, l + 2, 15:16, :] = radR[0, f * 4 + l : f * 4 + l + 1, :]
             X[f, l + 2, 12:13, :] = radR[1, f * 4 + l : f * 4 + l + 1, :]
 
-    def edge_lat(e):
-        return jnp.where(not_last, 0.1 / (e + next_lat(e)), 0.0)
-
     def edge_rad(e):
         return jnp.where(face_ok, 0.1 / (e + next_row(e)), 0.0)
 
     for p in range(1, 7):
         E[p] = jnp.exp(X[0, p])
     for p in range(2, 6):
-        QA[p] = edge_lat(E[p])
         QR[p] = edge_rad(E[p])
-    for p in range(1, 6):
+    for p in (1, 5):
         QO[p] = 0.1 / (E[p] + E[p + 1])
     load_1, load_2 = ice_ref[steps_ref[0]], ice_ref[steps_ref[1]]
     for f in range(3):
         for p in range(2, 6):
             u = X[f + 1, p]
-            flux = QA[p] * (next_lat(u) - u)
             rise = QR[p] * (next_row(u) - u)
-            total = u + (flux - last_lat(flux)) + (rise - last_row(rise))
-            total = total + QO[p] * (X[f + 1, p + 1] - u) + QO[p - 1] * (X[f + 1, p - 1] - u)
+            total = S1[f, p] + (rise - last_row(rise))
+            if p == 2:
+                total = total + QO[1] * (X[f + 1, 1] - u)
+            if p == 5:
+                total = total + QO[5] * (X[f + 1, 6] - u)
             if f == 0:
                 pressed = jnp.broadcast_to(load_1[p - 2 : p - 1, :], (16, NLAT)) * is_top
                 total = total - jnp.where(row == ROWS - 1, pressed, 0.0)

time: 55.2 us -> 54.7 us (level)
  no operation moved by 1% of the time
where the time goes in v5:
time: 54.7 us; the launch traced here: 54.5 us
  Pallas kernels  51.4 us (94%)
  between operations  2.41 us (4%)
  other arithmetic  0.73 us (1%)
    pallas_call x1, Pallas kernels, body(): pl.pallas_call(kernel, out_shape=(pltpu.VMEM((ROWS, COLS, NLAT), f32), ja...  51.4 us

profile of v5, /device:TPU:1, one launch (start us, length us, event | category | flops | bytes accessed | tf_op | source)
XLA Modules:
  0.0 54.5 jit_solution(3308013123397250745)
XLA Ops:
  0.6 0.0 copy-start
  0.6 0.0 copy-start.1
  0.7 51.4 %shard_map.103 = (f32[12,4,512]{2,1,0:T(4,128)S(1)}, f32[1]{0:T(128)}) custom-call(f32[12,4,512]{2,1,0:T(4,128)} %lv_hbm.1, f32[3,12,4,512]{3,2,1,0:T(4,128)} %u_hbm.1, f32[8,4,512]{2,1,0:T(4,128)} %ice_hbm.1, s32[2]{0:T(128)} %steps_ref.1, s32[1,12]{1,0:T(1,128)} %bitcast.1, f32[3,12]{1,0:T(4,128)} %observed_hbm.1, f32[3,12]{1,0:T(4,128)} %weight_hbm.1), custom_call_target="tpu_custom_call" | custom-call | tf_op jit(solution)/shard_map/pallas_call | solution.py:529
  52.0 0.0 copy-done
  52.1 0.0 copy-done.1
  52.1 0.7 %fusion = (f32[12,4,512]{2,1,0:T(4,128)}, f32[12,4,512]{2,1,0:T(4,128)}) fusion(f32[12,4,512]{2,1,0:T(4,128)S(1)} %copy-done, f32[12,4,512]{2,1,0:T(4,128)S(1)} %copy-done.1, f32[12,4,512]{2,1,0:T(4,128)S(1)} %get-tuple-element.5), kind=kLoop, calls=%fused_computation.1 | loop fusion | flops 73728 | bytes 491520 | tf_op jit(solution)/shard_map/add | solution.py:591
Async XLA Ops:
  0.6 51.4 %copy-start = (f32[12,4,512]{2,1,0:T(4,128)S(1)}, f32[12,4,512]{2,1,0:T(4,128)}, u32[]{:S(2)}) copy-start(f32[12,4,512]{2,1,0:T(4,128)} %lv_hbm.1) | copy-start | bytes 294916
  0.6 51.4 %copy-start.1 = (f32[12,4,512]{2,1,0:T(4,128)S(1)}, f32[12,4,512]{2,1,0:T(4,128)}, u32[]{:S(2)}) copy-start(f32[12,4,512]{2,1,0:T(4,128)} %param.9) | copy-start | bytes 294916

commit v6 on v5

--- a/solution.py
+++ b/solution.py
@@ -184,15 +184,19 @@
     pl.when(has_above)(lambda: send(radS.at[0], radR.at[0], ssem.at[0], rsem.at[0], above))
     pl.when(has_below)(lambda: send(radS.at[1], radR.at[1], ssem.at[1], rsem.at[1], below))
 
+    def send_edge(side):
+        target = (lax.rem(lon + 65 - 2 * side, 64), rad)
+        send(lonS.at[side, pl.ds(0, 48)], lonR.at[side, pl.ds(0, 48)], ssem.at[2 + side], rsem.at[2 + side], target)
+
+    send_edge(1 - c)
+
     def send_record(i):
         target, unused = z_peer((i + 12) % 16)
         send(packet, gathered.at[z % 8], ssem.at[4], rsem.at[4], target)
 
     repeat(0, 4, send_record)
     repeat(5, 8, send_record)
-    for side in (1 - c, c):
-        target = (lax.rem(lon + 65 - 2 * side, 64), rad)
-        send(lonS.at[side, pl.ds(0, 48)], lonR.at[side, pl.ds(0, 48)], ssem.at[2 + side], rsem.at[2 + side], target)
+    send_edge(c)
 
     row = iota((16, NLAT), 0)
     layer = jnp.where(row >= 14, row - 16, row)

time: 54.7 us -> 54.9 us (level)
  no operation moved by 1% of the time
where the time goes in v6:
time: 54.9 us; the launch traced here: 54.7 us
  Pallas kernels  51.6 us (94%)
  between operations  2.41 us (4%)
  other arithmetic  0.73 us (1%)
    pallas_call x1, Pallas kernels, body(): pl.pallas_call(kernel, out_shape=(pltpu.VMEM((ROWS, COLS, NLAT), f32), ja...  51.6 us

profile of v6, /device:TPU:1, one launch (start us, length us, event | category | flops | bytes accessed | tf_op | source)
XLA Modules:
  0.0 54.7 jit_solution(12678687715066617991)
XLA Ops:
  0.6 0.0 copy-start
  0.6 0.0 copy-start.1
  0.7 51.6 %shard_map.103 = (f32[12,4,512]{2,1,0:T(4,128)S(1)}, f32[1]{0:T(128)}) custom-call(f32[12,4,512]{2,1,0:T(4,128)} %lv_hbm.1, f32[3,12,4,512]{3,2,1,0:T(4,128)} %u_hbm.1, f32[8,4,512]{2,1,0:T(4,128)} %ice_hbm.1, s32[2]{0:T(128)} %steps_ref.1, s32[1,12]{1,0:T(1,128)} %bitcast.1, f32[3,12]{1,0:T(4,128)} %observed_hbm.1, f32[3,12]{1,0:T(4,128)} %weight_hbm.1), custom_call_target="tpu_custom_call" | custom-call | tf_op jit(solution)/shard_map/pallas_call | solution.py:533
  52.2 0.0 copy-done
  52.3 0.0 copy-done.1
  52.3 0.7 %fusion = (f32[12,4,512]{2,1,0:T(4,128)}, f32[12,4,512]{2,1,0:T(4,128)}) fusion(f32[12,4,512]{2,1,0:T(4,128)S(1)} %copy-done, f32[12,4,512]{2,1,0:T(4,128)S(1)} %copy-done.1, f32[12,4,512]{2,1,0:T(4,128)S(1)} %get-tuple-element.5), kind=kLoop, calls=%fused_computation.1 | loop fusion | flops 73728 | bytes 491520 | tf_op jit(solution)/shard_map/add | solution.py:595
Async XLA Ops:
  0.6 51.6 %copy-start = (f32[12,4,512]{2,1,0:T(4,128)S(1)}, f32[12,4,512]{2,1,0:T(4,128)}, u32[]{:S(2)}) copy-start(f32[12,4,512]{2,1,0:T(4,128)} %lv_hbm.1) | copy-start | bytes 294916
  0.6 51.6 %copy-start.1 = (f32[12,4,512]{2,1,0:T(4,128)S(1)}, f32[12,4,512]{2,1,0:T(4,128)}, u32[]{:S(2)}) copy-start(f32[12,4,512]{2,1,0:T(4,128)} %param.9) | copy-start | bytes 294916
